TPU v7x, 256 devices: a whole 4x4x8 slice. The times are simulated.
256 devices in a mesh: grp: 2 (over core), row: 16 (over y, x), col: 8 (over z).
Axes of the slice: x: 4, y: 4, z: 8, core: 2. Of those that a mesh axis runs over, the one named last changes fastest.
Arguments:
- raw_samples: bfloat16 [2, 8192, 2048], P(None, ('grp', 'row', 'col')), may hold values from -6 to 6
- window: float32 [2048], replicated, may hold values from 0.25 to 1.75
- steering: bfloat16 [8192, 2, 128], P(('grp', 'row', 'col')), may hold values from -0.375 to 0.375
- assignment: int32 [8192, 1], P(('grp', 'row', 'col')), may hold values from 0 to 15; in each aligned block of 32 rows (0 to 31, 32 to 63, ...) at most 6 rows name the same one
- beam_map: int32 [2, 2, 16, 2, 128], P(None, 'grp', 'row'), may hold values from 0 to 63
- interp_index: int32 [2, 2, 16, 2, 128], P(None, 'grp', 'row'), may hold values from 0 to 7
- phase_offset: float32 [2, 2, 16, 2, 128], P(None, 'grp', 'row'), may hold values from -3.140625 to 3.140625
- phase_rate: float32 [2, 2, 16, 2, 128], P(None, 'grp', 'row'), may hold values from -6 to 6
- interp_bank: bfloat16 [8, 128, 128], replicated, may hold values from -2 to 2
Outputs:
- image: bfloat16 [2, 16, 128, 2, 2048], P('grp', 'row', None, None, 'col')
Inputs may be any that keep to these rules, and one draw needn't show every extreme that they name: `assignment`: each pulse names an owner along row within its own half of grp; on every device at most 6 pulses name one owner, and on some device exactly 6 do.
All inputs are finite; a program needn't handle non-finite values.
Results may differ from a plain program's by a relative error of at most 0.007.
Values may be sent and summed in bfloat16 or wider, within the bound.
A program may use at most 64 MiB of HBM per device.

v0:
```python
import math

import jax
import jax.numpy as jnp
from jax import lax
from jax.sharding import PartitionSpec as P

NS = 2048
RT = 128
Q = 8


def from_partner(x, axis, bit):
    return lax.ppermute(x, axis, [(i, i ^ 1 << bit) for i in range(lax.axis_size(axis))])


def spectral_tables(window, samples):
    sample = jnp.arange(samples, dtype=jnp.int32)
    phase_index = sample[:, None] * sample[None, :] % samples
    phase_angle = phase_index.astype(jnp.float32) * (2.0 * math.pi / samples)
    scaling = window[:, None] / math.sqrt(samples)
    cos_table = (jnp.cos(phase_angle) * scaling).astype(jnp.bfloat16)
    sin_table = (jnp.sin(phase_angle) * scaling).astype(jnp.bfloat16)
    return jnp.concatenate([cos_table, sin_table], axis=1)


def interpolate(picked_rows, quants, offsets, rates, bank, positions):
    beam_count = picked_rows.shape[0]
    range_bins = picked_rows.shape[2]
    blocks = picked_rows.reshape(beam_count, 2, range_bins // RT, RT)
    all_phases = jnp.einsum("bctw,qwu->bctqu", blocks, bank, preferred_element_type=jnp.float32)
    chosen = all_phases[:, :, :, 0]
    for bank_index in range(1, Q):
        chosen = jnp.where(
            (quants == bank_index)[:, None, None, None], all_phases[:, :, :, bank_index], chosen
        )
    chosen = chosen.reshape(beam_count, 2, range_bins)
    phase_angle = offsets[:, None] + rates[:, None] * (positions[None, :] / NS)
    cosine = jnp.cos(phase_angle)
    sine_part = jnp.sin(phase_angle)
    real_part = chosen[:, 0] * cosine - chosen[:, 1] * sine_part
    imag_part = chosen[:, 0] * sine_part + chosen[:, 1] * cosine
    return jnp.stack([real_part, imag_part], axis=1)


def combine_halves(
    kept_half, partner_half, bit_value, maps, quants, offsets, rates, bank, positions
):
    low_half = jnp.where(bit_value == 0, kept_half, partner_half)
    high_half = jnp.where(bit_value == 0, partner_half, kept_half)
    first_term = interpolate(
        jnp.take(low_half, maps[0], axis=0), quants[0], offsets[0], rates[0], bank, positions
    )
    second_term = interpolate(
        jnp.take(high_half, maps[1], axis=0), quants[1], offsets[1], rates[1], bank, positions
    )
    return (first_term + second_term).astype(jnp.bfloat16)


def split_halves(image_share, bit_value):
    half_beams = image_share.shape[0] // 2
    kept_half = lax.dynamic_slice_in_dim(image_share, bit_value * half_beams, half_beams, 0)
    sent_half = lax.dynamic_slice_in_dim(image_share, (1 - bit_value) * half_beams, half_beams, 0)
    return (kept_half, sent_half)


def body(
    raw_samples,
    window,
    steering,
    assignment,
    beam_map,
    interp_index,
    phase_offset,
    phase_rate,
    interp_bank,
):
    col_count = lax.axis_size("col")
    row_count = lax.axis_size("row")
    pulse_count = raw_samples.shape[1]
    samples = raw_samples.shape[2]
    range_bins = samples // col_count
    beam_count = steering.shape[2]
    capacity = 3 * pulse_count // row_count
    spectral_table = spectral_tables(window, samples)
    product = jnp.dot(
        raw_samples.reshape(2 * pulse_count, samples),
        spectral_table,
        preferred_element_type=jnp.float32,
    )
    real_out = product[:pulse_count, :samples] + product[pulse_count:, samples:]
    imag_out = product[pulse_count:, :samples] - product[:pulse_count, samples:]
    compressed = jnp.stack(
        [
            real_out.reshape(pulse_count, col_count, range_bins),
            imag_out.reshape(pulse_count, col_count, range_bins),
        ],
        axis=2,
    ).astype(jnp.bfloat16)
    owner = assignment[:, 0]
    owner_table = (owner[:, None] == jnp.arange(row_count, dtype=jnp.int32)[None, :]).astype(
        jnp.int32
    )
    position = jnp.sum((jnp.cumsum(owner_table, axis=0) - 1) * owner_table, axis=1)
    pulse_ids = jnp.arange(pulse_count, dtype=jnp.int32)
    matches = (owner[:, None, None] == jnp.arange(row_count, dtype=jnp.int32)[None, :, None]) & (
        position[:, None, None] == jnp.arange(capacity, dtype=jnp.int32)[None, None, :]
    )
    found = jnp.any(matches, axis=0)
    source_pulse = jnp.sum(jnp.where(matches, pulse_ids[:, None, None], 0), axis=0)
    source_pulse = jnp.where(found, source_pulse, pulse_count)
    padded_pulses = jnp.concatenate(
        [compressed, jnp.zeros((1, col_count, 2, range_bins), jnp.bfloat16)], axis=0
    )
    flat_pulses = padded_pulses.reshape((pulse_count + 1) * col_count, 2, range_bins)
    flat_index = (
        source_pulse[:, None, :] * col_count + jnp.arange(col_count, dtype=jnp.int32)[None, :, None]
    )
    data_buffer = jnp.take(flat_pulses, flat_index, axis=0)
    padded_weights = jnp.concatenate(
        [steering, jnp.zeros((1, 2, beam_count), jnp.bfloat16)], axis=0
    )
    weight_rows = jnp.take(padded_weights, source_pulse, axis=0)
    weight_buffer = jnp.broadcast_to(
        weight_rows[:, None], (row_count, col_count, capacity, 2, beam_count)
    )
    got_data, got_weights = (
        lax.all_to_all(
            data_buffer.reshape(row_count * col_count, capacity, 2, range_bins),
            ("row", "col"),
            split_axis=0,
            concat_axis=0,
            tiled=True,
        ),
        lax.all_to_all(
            weight_buffer.reshape(row_count * col_count, capacity, 2, beam_count),
            ("row", "col"),
            split_axis=0,
            concat_axis=0,
            tiled=True,
        ),
    )
    data_slots = got_data.reshape(-1, 2, range_bins)
    weight_slots = got_weights.reshape(-1, 2, beam_count)
    partial_value = jnp.einsum(
        "sab,scr->abcr", weight_slots, data_slots, preferred_element_type=jnp.float32
    )
    image_zero = jnp.stack(
        [
            partial_value[0, :, 0] - partial_value[1, :, 1],
            partial_value[0, :, 1] + partial_value[1, :, 0],
        ],
        axis=1,
    ).astype(jnp.bfloat16)
    positions = (
        lax.axis_index("col") * range_bins + jnp.arange(range_bins, dtype=jnp.int32)
    ).astype(jnp.float32)
    core_bit = lax.axis_index("grp")
    kept_half, sent_half = split_halves(image_zero, core_bit)
    partner_half = from_partner(sent_half, "grp", 0)
    image_one = combine_halves(
        kept_half,
        partner_half,
        core_bit,
        beam_map[0, 0, 0],
        interp_index[0, 0, 0],
        phase_offset[0, 0, 0],
        phase_rate[0, 0, 0],
        interp_bank,
        positions,
    )
    row_bit = lax.axis_index("row") % 2
    kept_next, sent_next = split_halves(image_one, row_bit)
    partner_next = from_partner(sent_next, "row", 0)
    final_share = combine_halves(
        kept_next,
        partner_next,
        row_bit,
        beam_map[1, 0, 0],
        interp_index[1, 0, 0],
        phase_offset[1, 0, 0],
        phase_rate[1, 0, 0],
        interp_bank,
        positions,
    )
    return final_share[None, None]


def solution(mesh):
    in_specs = (
        P(None, ("grp", "row", "col"), None),
        P(),
        P(("grp", "row", "col"), None, None),
        P(("grp", "row", "col"), None),
        P(None, "grp", "row", None, None),
        P(None, "grp", "row", None, None),
        P(None, "grp", "row", None, None),
        P(None, "grp", "row", None, None),
        P(),
    )
    out_specs = P("grp", "row", None, None, "col")
    return jax.shard_map(body, mesh=mesh, in_specs=in_specs, out_specs=out_specs, check_vma=False)
```

profile of v0, /device:TPU:1, one launch (start us, length us, event | category | flops | bytes accessed | tf_op | source)
XLA Modules:
  0.0 198.5 jit_solution(8618310208788866079)
XLA Ops:
  0.8 0.8 select_reduce_fusion
  4.0 1.2 copy.206
  5.1 16.3 %all-to-all-start = ((bf16[128,6,2,128]{3,2,1,0:T(2,128)(2,1)}), bf16[128,6,2,128]{3,2,1,0:T(2,128)(2,1)S(1)}, u32[]{:S(2)}, u32[]{:S(2)}) async-start(bf16[128,6,2,128]{3,2,1,0:T(2,128)(2,1)} %copy.206), calls=%async_computation | async-start | bytes 786432 | tf_op jit(solution)/shard_map/all_to_all | solution.py:135
  22.2 68.2 %multiply_convert_fusion.1 = (bf16[2048,2048]{1,0:T(8,128)(2,1)S(1)}, bf16[2048,2048]{1,0:T(8,128)(2,1)S(1)}) fusion(f32[2048]{0:T(1024)S(1)} %broadcast_multiply_fusion), kind=kLoop, calls=%fused_computation.17 | loop fusion | flops 75497472 | bytes 16785408 | tf_op jit(solution)/shard_map/convert_element_type | solution.py:22
  90.4 3.1 %fusion.10 = f32[64,4096]{1,0:T(8,128)S(1)} fusion(bf16[64,2048]{1,0:T(8,128)(2,1)S(1)} %bitcast.225, bf16[2048,2048]{1,0:T(8,128)(2,1)S(1)} %get-tuple-element.63, bf16[2048,2048]{1,0:T(8,128)(2,1)S(1)} %get-tuple-element.62), kind=kOutput, calls=%fused_computation.21 | convolution fusion | flops 1107296256 | bytes 18087936 | tf_op jit(solution)/shard_map/dot_general | solution.py:86
  94.8 3.6 %gather_fusion.1 = bf16[768,2,256]{2,1,0:T(2,128)(2,1)S(1)} fusion(bf16[264,2,256]{2,1,0:T(2,128)(2,1)S(1)} %bitcast.179, s32[1024]{0:T(1024)S(1)} %pad_clamp_fusion.4), kind=kCustom, calls=%fused_computation.5 | custom fusion | bytes 1575936 | tf_op jit(solution)/shard_map/jit(_take)/gather | solution.py:119
  98.4 2.3 %broadcast_select_fusion = bf16[128,6,2,256]{3,2,1,0:T(2,128)(2,1)} fusion(bf16[128,6,2,256]{3,2,1,0:T(2,128)(2,1)S(1)} %bitcast.180, pred[128,6]{1,0:T(8,128)(4,1)S(1)} %copy.207), kind=kLoop, calls=%fused_computation.22 | loop fusion | flops 393216 | bytes 1573632 | tf_op jit(solution)/shard_map/jit(_take)/select_n | solution.py:119
  100.7 13.4 %all-to-all-start.1 = ((bf16[128,6,2,256]{3,2,1,0:T(2,128)(2,1)}), bf16[128,6,2,256]{3,2,1,0:T(2,128)(2,1)S(1)}, u32[]{:S(2)}, u32[]{:S(2)}) async-start(bf16[128,6,2,256]{3,2,1,0:T(2,128)(2,1)} %broadcast_select_fusion), calls=%async_computation.1 | async-start | bytes 1572864 | tf_op jit(solution)/shard_map/all_to_all | solution.py:128
  116.7 21.3 %all-to-all-done.1 = bf16[128,6,2,256]{3,2,1,0:T(2,128)(2,1)S(1)} async-done(((bf16[128,6,2,256]{3,2,1,0:T(2,128)(2,1)}), bf16[128,6,2,256]{3,2,1,0:T(2,128)(2,1)S(1)}, u32[]{:S(2)}, u32[]{:S(2)}) %all-to-all-start.1) | async-done | bytes 786464 | tf_op jit(solution)/shard_map/all_to_all | solution.py:128
  138.5 3.3 %collective-permute-start = (bf16[64,2,256]{2,0,1:T(8,128)(2,1)S(1)}, bf16[64,2,256]{2,0,1:T(8,128)(2,1)S(1)}, u32[]{:S(2)}, u32[]{:S(2)}) collective-permute-start(bf16[64,2,256]{2,0,1:T(8,128)(2,1)S(1)} %fusion.44), channel_id=1, source_target_pairs={{0,128},{128,0},{1,129},{129,1},{2,130},{130,2},{3,131},{131,3},{4... | collective-permute-start | bytes 196616 | tf_op jit(solution)/shard_map/ppermute | solution.py:14
  141.8 0.9 collective-permute-done
  142.8 0.9 gather_fusion.3
  145.4 0.8 copy.229
  147.0 0.8 copy.226
  147.9 0.8 copy.227
  148.8 0.9 gather_fusion.2
  150.7 0.8 copy.222
  152.6 2.9 %select_select_fusion.2 = f32[128,2,256]{2,1,0:T(2,128)S(1)} fusion(f32[128,2,256]{2,1,0:T(2,128)S(1)} %copy.233, f32[128,2,256]{2,1,0:T(2,128)S(1)} %copy.232, f32[128,2,256]{2,1,0:T(2,128)S(1)} %copy.231, f32[128,2,256]{2,1,0:T(2,128)S(1)} %copy.230, f32[128,2,256]{2,1,0:T(2,128)} %copy.229, f32[128,2,256]{2,1,0:T(2,128)} %copy.228, ...), kind=kLoop, calls=%fused_computation.46 | loop fusion | flops 458752 | bytes 2360192 | tf_op jit(solution)/shard_map/jit(_where)/select_n | solution.py:34
  155.6 2.7 %select_select_fusion.3 = f32[128,2,256]{2,1,0:T(2,128)S(1)} fusion(f32[128,2,256]{2,1,0:T(2,128)} %copy.222, f32[128,2,256]{2,1,0:T(2,128)S(1)} %copy.221, f32[128,2,256]{2,1,0:T(2,128)S(1)} %copy.220, f32[128,2,256]{2,1,0:T(2,128)S(1)} %copy.219, f32[128,2,256]{2,1,0:T(2,128)S(1)} %copy.218, f32[128,2,256]{2,1,0:T(2,128)S(1)} %copy.217, ...), kind=kLoop, calls=%fused_computation.47 | loop fusion | flops 458752 | bytes 2360192 | tf_op jit(solution)/shard_map/jit(_where)/select_n | solution.py:34
  158.3 9.0 %multiply_subtract_fusion = (f32[128,1,256]{2,1,0:T(1,128)S(1)}, f32[128,1,256]{2,1,0:T(1,128)S(1)}, f32[128,1,256]{2,1,0:T(1,128)S(1)}, f32[128,1,256]{2,1,0:T(1,128)S(1)}) fusion(f32[128,2,256]{2,1,0:T(2,128)S(1)} %select_select_fusion.2, f32[256]{0:T(256)S(1)} %convert_multiply_fusion, f32[128]{0:T(128)S(1)} %get-tuple-element.69, ...), kind=kLoop, calls=%fused_computation.73 | loop fusion | flops 524288 | bytes 1051648 | tf_op jit(solution)/shard_map/sub | solution.py:41
  168.1 3.1 %collective-permute-done.1 = bf16[64,2,256]{2,1,0:T(2,128)(2,1)S(1)} collective-permute-done((bf16[64,2,256]{2,1,0:T(2,128)(2,1)S(1)}, bf16[64,2,256]{2,1,0:T(2,128)(2,1)S(1)}, u32[]{:S(2)}, u32[]{:S(2)}) %collective-permute-start.1) | collective-permute-done | bytes 65568 | tf_op jit(solution)/shard_map/ppermute | solution.py:14
  171.3 0.9 gather_fusion.5
  172.2 0.9 gather_fusion.4
  173.1 1.3 broadcast_select_fusion.1
  176.7 0.8 copy.248
  177.5 0.8 copy.246
  178.3 0.8 copy.247
  180.0 0.8 copy.243
  181.9 3.0 %select_select_fusion = f32[128,2,256]{2,1,0:T(2,128)S(1)} fusion(f32[128,2,256]{2,1,0:T(2,128)S(1)} %copy.253, f32[128,2,256]{2,1,0:T(2,128)S(1)} %copy.252, f32[128,2,256]{2,1,0:T(2,128)S(1)} %copy.251, f32[128,2,256]{2,1,0:T(2,128)S(1)} %copy.250, f32[128,2,256]{2,1,0:T(2,128)} %copy.249, f32[128,2,256]{2,1,0:T(2,128)} %copy.248, ...), kind=kLoop, calls=%fused_computation.44 | loop fusion | flops 458752 | bytes 2360192 | tf_op jit(solution)/shard_map/jit(_where)/select_n | solution.py:34
  184.9 2.8 %select_select_fusion.1 = f32[128,2,256]{2,1,0:T(2,128)S(1)} fusion(f32[128,2,256]{2,1,0:T(2,128)} %copy.243, f32[128,2,256]{2,1,0:T(2,128)S(1)} %copy.242, f32[128,2,256]{2,1,0:T(2,128)S(1)} %copy.241, f32[128,2,256]{2,1,0:T(2,128)S(1)} %copy.240, f32[128,2,256]{2,1,0:T(2,128)S(1)} %copy.239, f32[128,2,256]{2,1,0:T(2,128)S(1)} %copy.238, ...), kind=kLoop, calls=%fused_computation.45 | loop fusion | flops 458752 | bytes 2360192 | tf_op jit(solution)/shard_map/jit(_where)/select_n | solution.py:34
  187.7 9.8 %subtract_bitcast_fusion = (f32[1,1,128,1,256]{4,3,2,1,0:T(1,128)S(1)}, f32[1,1,128,1,256]{4,3,2,1,0:T(1,128)S(1)}, f32[1,1,128,1,256]{4,3,2,1,0:T(1,128)S(1)}, f32[1,1,128,1,256]{4,3,2,1,0:T(1,128)S(1)}) fusion(f32[128,2,256]{2,1,0:T(2,128)S(1)} %select_select_fusion, f32[256]{0:T(256)S(1)} %convert_multiply_fusion, f32[128]{0:T(128)S(1)} %get-tuple-element.68, ...), kind=kLoop, calls=%fused_computation.67 | loop fusion | flops 524288 | bytes 1051648 | tf_op jit(solution)/shard_map/stack | solution.py:43
  197.4 1.1 fusion.19
  (104 shorter events, 17.6 us)
Async XLA Ops:
  0.0 144.0 %copy-start = (bf16[8,128,128]{2,1,0:T(8,128)(2,1)S(1)}, bf16[8,128,128]{2,1,0:T(8,128)(2,1)}, u32[]{:S(2)}) copy-start(bf16[8,128,128]{2,1,0:T(8,128)(2,1)} %param.19) | copy-start | bytes 786436
  5.1 95.6 %all-to-all-start = ((bf16[128,6,2,128]{3,2,1,0:T(2,128)(2,1)}), bf16[128,6,2,128]{3,2,1,0:T(2,128)(2,1)S(1)}, u32[]{:S(2)}, u32[]{:S(2)}) async-start(bf16[128,6,2,128]{3,2,1,0:T(2,128)(2,1)} %copy.206), calls=%async_computation | async-start | bytes 786432 | tf_op jit(solution)/shard_map/all_to_all | solution.py:135
  22.2 68.2 %copy-start.5 = (bf16[2,32,2048]{2,1,0:T(8,128)(2,1)S(1)}, bf16[2,32,2048]{2,1,0:T(8,128)(2,1)}, u32[]{:S(2)}) copy-start(bf16[2,32,2048]{2,1,0:T(8,128)(2,1)} %param.11) | copy-start | bytes 786436
  93.5 20.7 %copy-start.2 = (s32[2,1,1,2,128]{4,3,2,1,0:T(2,128)S(1)}, s32[2,1,1,2,128]{4,3,2,1,0:T(2,128)}, u32[]{:S(2)}) copy-start(s32[2,1,1,2,128]{4,3,2,1,0:T(2,128)} %param.15) | copy-start | bytes 6148
  93.5 21.4 %copy-start.3 = (f32[2,1,1,2,128]{4,3,2,1,0:T(2,128)S(1)}, f32[2,1,1,2,128]{4,3,2,1,0:T(2,128)}, u32[]{:S(2)}) copy-start(f32[2,1,1,2,128]{4,3,2,1,0:T(2,128)} %param.18) | copy-start | bytes 6148
  93.5 21.4 %copy-start.4 = (f32[2,1,1,2,128]{4,3,2,1,0:T(2,128)S(1)}, f32[2,1,1,2,128]{4,3,2,1,0:T(2,128)}, u32[]{:S(2)}) copy-start(f32[2,1,1,2,128]{4,3,2,1,0:T(2,128)} %param.17) | copy-start | bytes 6148
  93.5 22.0 %copy-start.1 = (s32[2,1,1,2,128]{4,3,2,1,0:T(2,128)S(1)}, s32[2,1,1,2,128]{4,3,2,1,0:T(2,128)}, u32[]{:S(2)}) copy-start(s32[2,1,1,2,128]{4,3,2,1,0:T(2,128)} %param.16) | copy-start | bytes 6148
  100.7 37.3 %all-to-all-start.1 = ((bf16[128,6,2,256]{3,2,1,0:T(2,128)(2,1)}), bf16[128,6,2,256]{3,2,1,0:T(2,128)(2,1)S(1)}, u32[]{:S(2)}, u32[]{:S(2)}) async-start(bf16[128,6,2,256]{3,2,1,0:T(2,128)(2,1)} %broadcast_select_fusion), calls=%async_computation.1 | async-start | bytes 1572864 | tf_op jit(solution)/shard_map/all_to_all | solution.py:128
  138.5 4.2 %collective-permute-start = (bf16[64,2,256]{2,0,1:T(8,128)(2,1)S(1)}, bf16[64,2,256]{2,0,1:T(8,128)(2,1)S(1)}, u32[]{:S(2)}, u32[]{:S(2)}) collective-permute-start(bf16[64,2,256]{2,0,1:T(8,128)(2,1)S(1)} %fusion.44), channel_id=1, source_target_pairs={{0,128},{128,0},{1,129},{129,1},{2,130},{130,2},{3,131},{131,3},{4... | collective-permute-start | bytes 196616 | tf_op jit(solution)/shard_map/ppermute | solution.py:14
  167.8 3.4 %collective-permute-start.1 = (bf16[64,2,256]{2,1,0:T(2,128)(2,1)S(1)}, bf16[64,2,256]{2,1,0:T(2,128)(2,1)S(1)}, u32[]{:S(2)}, u32[]{:S(2)}) collective-permute-start(bf16[64,2,256]{2,1,0:T(2,128)(2,1)S(1)} %constant_dynamic-slice_fusion), channel_id=1, source_target_pairs={{0,8},{8,0},{16,24},{24,16},{32,40},{40,32},{48,56},{56,48},{64,72... | collective-permute-start | bytes 196616 | tf_op jit(solution)/shard_map/ppermute | solution.py:14
where the time goes:
time: 199 us
  other arithmetic  109 us (55%)
  starting transfers between devices  33.4 us (17%)
  waiting for transfers between devices  25.3 us (13%)
  local copies, waits for them, and re-layouts  24.8 us (12%)
  matrix products  5.37 us (3%)
    convert_element_type x1, other arithmetic, spectral_tables(): cos_table = (jnp.cos(phase_angle) * scaling).astype(jnp.bfloat16)  68.2 us
    all_to_all x1, waiting for transfers between devices, body(): lax.all_to_all(data_buffer.reshape(row_count * col_count, capacity, 2, ra...  21.3 us
    all_to_all x1, starting transfers between devices, body(): lax.all_to_all(weight_buffer.reshape(row_count * col_count, capacity, 2,...  16.3 us
    all_to_all x1, starting transfers between devices, body(): lax.all_to_all(data_buffer.reshape(row_count * col_count, capacity, 2, ra...  13.4 us
    select_n x4, other arithmetic, interpolate(): jnp.where((quants == bank_index)[:, None, None, None], all_phases[:, :, :...  11.4 us
    another operation x1, other arithmetic, interpolate(): return jnp.stack([real_part, imag_part], axis=1)  9.75 us
    squeeze x28, local copies, waits for them, and re-layouts, interpolate(): all_phases[:, :, :, bank_index]  9.68 us
    sub x1, other arithmetic, interpolate(): real_part = chosen[:, 0] * cosine - chosen[:, 1] * sine_part  9.01 us
  transfers between devices with their start and end apart: 4, of which 3 were waited for; matrix products, arithmetic and copies ran while one was open for 41% of the time, Pallas kernels for 0%

commit v1 on v0

v1 whole, which is shorter than its diff:
```python
import math

import jax
import jax.numpy as jnp
from jax import lax
from jax.experimental import pallas as pl
from jax.experimental.pallas import tpu as pltpu
from jax.sharding import PartitionSpec as P

MESH = pl.DeviceIdType.MESH
F32, BF16, I32 = jnp.float32, jnp.bfloat16, jnp.int32

NS = 2048
BEAMS = 128
RT = 128
Q = 8
P_DEV = 32
CAP = 6
ROWS = 16
COLS = 8
SLOTS = COLS * CAP
HALF = BEAMS // 2
CHUNKS = 2

COS = (
    0.9999999890590227,
    -19.73920449945391,
    64.93911745989556,
    -85.45013953088247,
    60.16763095094928,
    -25.967599248494622,
    6.528658161366808,
)
SIN = (
    6.283185302511503,
    -41.341700405317496,
    81.60513138579344,
    -76.70301535379849,
    42.025926985567956,
    -14.89984666736486,
    3.238137509743233,
)


def horner(coefs, y):
    total = jnp.full_like(y, coefs[-1])
    for c in coefs[-2::-1]:
        total = total * y + c
    return total


def cos_sin(turns):
    r = turns - jnp.floor(turns + 0.5)
    y = r * r
    return horner(COS, y), horner(SIN, y) * r


def dft8(xr, xi):
    h = math.sqrt(0.5)
    ur = [xr[j] + xr[j + 4] for j in range(4)]
    ui = [xi[j] + xi[j + 4] for j in range(4)]
    vr = [xr[j] - xr[j + 4] for j in range(4)]
    vi = [xi[j] - xi[j + 4] for j in range(4)]
    wr = [vr[0], (vr[1] + vi[1]) * h, vi[2], (vi[3] - vr[3]) * h]
    wi = [vi[0], (vi[1] - vr[1]) * h, -vr[2], (-vr[3] - vi[3]) * h]
    yr, yi = [None] * 8, [None] * 8
    for odd, (zr, zi) in enumerate(((ur, ui), (wr, wi))):
        ar, ai = zr[0] + zr[2], zi[0] + zi[2]
        br, bi = zr[0] - zr[2], zi[0] - zi[2]
        cr, ci = zr[1] + zr[3], zi[1] + zi[3]
        dr, di = zr[1] - zr[3], zi[1] - zi[3]
        yr[odd], yi[odd] = ar + cr, ai + ci
        yr[odd + 4], yi[odd + 4] = ar - cr, ai - ci
        yr[odd + 2], yi[odd + 2] = br + di, bi - dr
        yr[odd + 6], yi[odd + 6] = br - di, bi + dr
    return yr, yi


def swap_groups(tiles):
    group = lax.broadcasted_iota(I32, tiles[0].shape, 1) // 16
    tiles = list(tiles)
    for bit in range(3):
        step = 1 << bit
        upper = (group // step) % 2 == 1
        for a in range(8):
            if a & step:
                continue
            low, high = tiles[a], tiles[a + step]
            tiles[a] = jnp.where(upper, pltpu.roll(high, 16 * step, 1), low)
            tiles[a + step] = jnp.where(upper, high, pltpu.roll(low, 128 - 16 * step, 1))
    return tiles


def dot(a, b):
    return jnp.dot(a, b, preferred_element_type=F32)


def iota(shape, dim):
    return lax.broadcasted_iota(I32, shape, dim)


def kernel(
    raw,
    window,
    steering,
    assignment,
    beam_map,
    interp_index,
    phase_offset,
    phase_rate,
    bank,
    out,
    ybuf,
    table,
    twiddle,
    st_own,
    st_all,
    code_own,
    code_all,
    dsend,
    zall,
    sel,
    slots,
    got,
    weights_t,
    par,
    bank_nat,
    bank_perm,
    picks,
    cosb,
    sinb,
    img,
    child,
    vbuf,
    outf,
    st_send,
    st_recv,
    code_send,
    code_recv,
    z_send,
    z_recv,
    r_send,
    r_recv,
    x_send,
    x_recv,
):
    g, row, col = lax.axis_index("grp"), lax.axis_index("row"), lax.axis_index("col")
    ry, rx = row // 4, row % 4

    def remote(src, dst, ssem, rsem, device):
        return pltpu.make_async_remote_copy(
            src_ref=src,
            dst_ref=dst,
            send_sem=ssem,
            recv_sem=rsem,
            device_id=device,
            device_id_type=MESH,
        )

    barrier = pltpu.get_barrier_semaphore()

    def greet_col(i, _):
        pl.semaphore_signal(
            barrier, inc=1, device_id=(g, row, (col + i) % COLS), device_id_type=MESH
        )
        return 0

    def greet_row(i, _):
        pl.semaphore_signal(
            barrier, inc=1, device_id=(g, (row + i) % ROWS, col), device_id_type=MESH
        )
        return 0

    lax.fori_loop(1, COLS, greet_col, 0)
    lax.fori_loop(1, ROWS, greet_row, 0)
    pl.semaphore_signal(barrier, inc=1, device_id=(1 - g, row, col), device_id_type=MESH)

    own_row = assignment[...].astype(F32)
    eye = iota((P_DEV, P_DEV), 0) == iota((P_DEV, P_DEV), 1)
    before = iota((P_DEV, P_DEV), 1) < iota((P_DEV, P_DEV), 0)
    own_col = jnp.sum(jnp.where(eye, own_row, 0.0), axis=1, keepdims=True)
    rank = jnp.sum(
        jnp.where(before & (own_col == own_row), 1.0, 0.0), axis=1, keepdims=True
    )
    code_col = own_col * SLOTS + rank + (col * CAP).astype(F32)
    place = iota((P_DEV, 128), 0) + 32 * (col % 4)
    code = jnp.sum(
        jnp.where(iota((P_DEV, 128), 1) == place, code_col, 0.0), axis=0, keepdims=True
    )
    code_own[...] = jnp.broadcast_to(code, (8, 128))

    pick = iota((2 * P_DEV, 2 * P_DEV), 0)
    pick = (pick % P_DEV) * 2 + pick // P_DEV == iota((2 * P_DEV, 2 * P_DEV), 1)
    parts = dot(pick.astype(F32).astype(BF16), steering[...]).astype(BF16)
    st_own[:, :BEAMS] = parts[:P_DEV]
    st_own[:, BEAMS:] = parts[P_DEV:]

    pl.semaphore_wait(barrier, COLS - 1 + ROWS - 1 + 1)

    first_sends = []
    for i in range(1, COLS):
        dest = (col + i) % COLS
        device = (g, row, dest)
        mine = pl.ds(pl.multiple_of(col * P_DEV, P_DEV), P_DEV)
        c1 = remote(code_own, code_all.at[col], code_send.at[i], code_recv.at[col], device)
        c2 = remote(st_own, st_all.at[mine], st_send.at[i], st_recv.at[col], device)
        c1.start()
        c2.start()
        first_sends += [c1, c2]
    code_all[col] = code_own[...]
    st_all[pl.ds(pl.multiple_of(col * P_DEV, P_DEV), P_DEV), :] = st_own[...]

    steps = (iota((8, 256), 0) * iota((8, 256), 1)).astype(F32) * (1.0 / NS)
    tc, ts = cos_sin(steps)
    twiddle[0] = tc
    twiddle[1] = ts
    for m in range(CHUNKS):
        lane = iota((256, 128), 1)
        d = (lane // 16) * 32 + 16 * m + lane % 16
        turns = ((iota((256, 128), 0) * d) % 256).astype(F32) * (1.0 / 256)
        c, s = cos_sin(turns)
        c, s = c.astype(BF16), s.astype(BF16)
        table[m, :256, :128] = c
        table[m, :256, 128:] = -s
        table[m, 256:, :128] = s
        table[m, 256:, 128:] = c

    scale = 1.0 / math.sqrt(NS)
    for lh in range(2):
        lanes = [pl.ds(256 * t + 128 * lh, 128) for t in range(8)]
        taper = [window[:, lanes[t]] * scale for t in range(8)]
        for pg in range(P_DEV // 16):
            rows = pl.ds(16 * pg, 16)
            xr = [raw[0, rows, lanes[t]].astype(F32) * taper[t] for t in range(8)]
            xi = [raw[1, rows, lanes[t]].astype(F32) * taper[t] for t in range(8)]
            yr, yi = dft8(xr, xi)
            for c in range(8):
                zr, zi = yr[c], yi[c]
                if c:
                    wc = twiddle[0, c : c + 1, 128 * lh : 128 * lh + 128]
                    ws = twiddle[1, c : c + 1, 128 * lh : 128 * lh + 128]
                    zr, zi = zr * wc + zi * ws, zi * wc - zr * ws
                to = pl.ds(P_DEV * c + 16 * pg, 16)
                ybuf[to, 128 * lh : 128 * lh + 128] = zr.astype(BF16)
                ybuf[to, 256 + 128 * lh : 256 + 128 * lh + 128] = zi.astype(BF16)

    z_sends = []
    for m in range(CHUNKS):
        spectrum = dot(ybuf[...], table[m])
        for part in range(2):
            tiles = swap_groups(
                [
                    spectrum[P_DEV * c : P_DEV * c + P_DEV, 128 * part : 128 * part + 128]
                    for c in range(8)
                ]
            )
            for c in range(8):
                dsend[m, c, :, 128 * part : 128 * part + 128] = tiles[c].astype(BF16)
        mine = pl.ds(pl.multiple_of(col * P_DEV, P_DEV), P_DEV)
        for i in range(1, COLS):
            dest = (col + i) % COLS
            c1 = remote(
                dsend.at[m, dest],
                zall.at[m, mine],
                z_send.at[m, i],
                z_recv.at[m, col],
                (g, row, dest),
            )
            c1.start()
            z_sends.append(c1)
        zall[m, mine, :] = dsend[m, col]

    def from_cols(wait):
        for i in range(1, COLS):
            wait((col + i) % COLS)

    def wait_first(source):
        at = pl.ds(pl.multiple_of(source * P_DEV, P_DEV), P_DEV)
        remote(
            code_own, code_all.at[source], code_send.at[0], code_recv.at[source], (g, row, source)
        ).wait_recv()
        remote(
            st_own, st_all.at[at], st_send.at[0], st_recv.at[source], (g, row, source)
        ).wait_recv()

    from_cols(wait_first)
    low = code_all[0] + code_all[1] + code_all[2] + code_all[3]
    high = code_all[4] + code_all[5] + code_all[6] + code_all[7]
    codes = jnp.concatenate([low[:1], high[:1]], axis=1).astype(I32)
    for y in range(4):
        sel[192 * y : 192 * y + 192] = jnp.where(
            iota((192, 256), 0) + 192 * y == codes, 1.0, 0.0
        ).astype(BF16)

    row_sends = []

    def to_owners(kind, data):
        mine = pl.ds(pl.multiple_of(row * SLOTS, SLOTS), SLOTS)
        for dy in (2, 1, 3, 0):
            y = (ry + dy) % 4
            block = pl.ds(pl.multiple_of(y * 4 * SLOTS, 4 * SLOTS), 4 * SLOTS)
            slots[kind, block, :] = dot(sel[block, :], data[...]).astype(BF16)
            for dx in (2, 1, 3, 0):
                dest = y * 4 + (rx + dx) % 4
                there = pl.ds(pl.multiple_of(dest * SLOTS, SLOTS), SLOTS)
                if dy == 0 and dx == 0:
                    got[kind, mine, :] = slots[kind, mine, :]
                    continue
                c1 = remote(
                    slots.at[kind, there],
                    got.at[kind, mine],
                    r_send.at[kind, 4 * dy + dx],
                    r_recv.at[kind, row],
                    (g, dest, col),
                )
                c1.start()
                row_sends.append(c1)

    def from_rows(kind):
        for i in range(1, ROWS):
            source = (row + i) % ROWS
            at = pl.ds(pl.multiple_of(source * SLOTS, SLOTS), SLOTS)
            remote(
                slots.at[kind, at],
                got.at[kind, at],
                r_send.at[kind, 0],
                r_recv.at[kind, source],
                (g, source, col),
            ).wait_recv()

    to_owners(2, st_all)

    for m in range(CHUNKS):

        def wait_z(source):
            at = pl.ds(pl.multiple_of(source * P_DEV, P_DEV), P_DEV)
            remote(
                dsend.at[m, 0],
                zall.at[m, at],
                z_send.at[m, 0],
                z_recv.at[m, source],
                (g, row, source),
            ).wait_recv()

        from_cols(wait_z)
        to_owners(m, zall.at[m])

    par[...] = jnp.zeros_like(par)
    par[0:4, :] = (interp_index[...] * HALF + beam_map[...]).astype(F32)
    par[8:12, :] = phase_offset[...]
    par[16:20, :] = phase_rate[...]
    columns = par[...].T
    bins = (col * 256 + iota((1, 256), 1)).astype(F32) * (1.0 / NS)
    for ls in range(4):
        code = columns[:, ls : ls + 1].astype(I32)
        picks[ls] = jnp.where(iota((BEAMS, Q * HALF), 1) == code, 1.0, 0.0).astype(BF16)
        angle = columns[:, 8 + ls : 9 + ls] + columns[:, 16 + ls : 17 + ls] * bins
        c, s = cos_sin(angle * (0.5 / math.pi))
        cosb[ls] = c
        sinb[ls] = s
    for q in range(Q):
        bank_nat[:, RT * q : RT * q + RT] = bank[RT * q : RT * q + RT, :]
    lane = iota((RT, RT), 0)
    order = ((lane % 16) * 8 + lane // 16 == iota((RT, RT), 1)).astype(F32).astype(BF16)
    bank_perm[...] = dot(order, bank_nat[...]).astype(BF16)

    from_rows(2)
    weights_t[...] = got[2].T

    def merge(level, m, matrices):
        lhs = jnp.concatenate(
            [child[level, m, s, :, 128 * part : 128 * part + 128] for s in range(2) for part in range(2)],
            axis=0,
        )
        v = dot(lhs, matrices[...]).astype(BF16)
        total = None
        for s in range(2):
            for part in range(2):
                at = (2 * s + part) * HALF
                for q in range(Q):
                    vbuf[s, HALF * q : HALF * q + HALF, 128 * part : 128 * part + 128] = v[
                        at : at + HALF, RT * q : RT * q + RT
                    ]
            t = dot(picks[2 * level + s], vbuf[s])
            tr, ti = t[:, :128], t[:, 128:]
            c = cosb[2 * level + s, :, 128 * m : 128 * m + 128]
            d = sinb[2 * level + s, :, 128 * m : 128 * m + 128]
            yr, yi = tr * c - ti * d, tr * d + ti * c
            total = (yr, yi) if total is None else (total[0] + yr, total[1] + yi)
        return total

    def exchange(level, m, real, imag, bit, device):
        img[level, m, :, :128] = real.astype(BF16)
        img[level, m, :, 128:] = imag.astype(BF16)
        keep = pl.ds(pl.multiple_of(bit * HALF, HALF), HALF)
        give = pl.ds(pl.multiple_of((1 - bit) * HALF, HALF), HALF)
        c1 = remote(
            img.at[level, m, give],
            child.at[level, m, bit],
            x_send.at[level, m],
            x_recv.at[level, m],
            device,
        )
        c1.start()
        child[level, m, bit] = img[level, m, keep, :]
        return c1

    def arrive(level, m, bit, device):
        remote(
            img.at[level, m, 0:HALF],
            child.at[level, m, 1 - bit],
            x_send.at[level, m],
            x_recv.at[level, m],
            device,
        ).wait_recv()

    sibling = (1 - g, row, col)
    v = row % 2
    partner = (g, row + 1 - 2 * v, col)
    x_sends = []
    for m in range(CHUNKS):
        from_rows(m)
        a = dot(weights_t[...], got[m])
        x_sends.append(
            exchange(
                0,
                m,
                a[:BEAMS, :128] - a[BEAMS:, 128:],
                a[:BEAMS, 128:] + a[BEAMS:, :128],
                g,
                sibling,
            )
        )
        arrive(0, m, g, sibling)
        real, imag = merge(0, m, bank_perm)
        x_sends.append(exchange(1, m, real, imag, v, partner))
    for m in range(CHUNKS):
        arrive(1, m, v, partner)
        real, imag = merge(1, m, bank_nat)
        outf[pl.ds(2 * m, BEAMS, stride=4), :] = real
        outf[pl.ds(2 * m + 1, BEAMS, stride=4), :] = imag
    out[...] = outf[...].astype(BF16)

    for c1 in first_sends + z_sends + row_sends + x_sends:
        c1.wait_send()


def body(
    raw_samples,
    window,
    steering,
    assignment,
    beam_map,
    interp_index,
    phase_offset,
    phase_rate,
    interp_bank,
):
    dma = pltpu.SemaphoreType.DMA
    vmem = pltpu.VMEM
    out = pl.pallas_call(
        kernel,
        out_shape=jax.ShapeDtypeStruct((4 * BEAMS, 128), BF16),
        in_specs=[pl.BlockSpec(memory_space=pltpu.VMEM)] * 9,
        out_specs=pl.BlockSpec(memory_space=pltpu.VMEM),
        scratch_shapes=[
            vmem((8 * P_DEV, 512), BF16),
            vmem((CHUNKS, 512, 256), BF16),
            vmem((2, 8, 256), F32),
            vmem((P_DEV, 256), BF16),
            vmem((COLS * P_DEV, 256), BF16),
            vmem((8, 128), F32),
            vmem((COLS, 8, 128), F32),
            vmem((CHUNKS, COLS, P_DEV, 256), BF16),
            vmem((CHUNKS, COLS * P_DEV, 256), BF16),
            vmem((ROWS * SLOTS, 256), BF16),
            vmem((3, ROWS * SLOTS, 256), BF16),
            vmem((3, ROWS * SLOTS, 256), BF16),
            vmem((256, ROWS * SLOTS), BF16),
            vmem((128, 128), F32),
            vmem((RT, Q * RT), BF16),
            vmem((RT, Q * RT), BF16),
            vmem((4, BEAMS, Q * HALF), BF16),
            vmem((4, BEAMS, 256), F32),
            vmem((4, BEAMS, 256), F32),
            vmem((2, CHUNKS, BEAMS, 256), BF16),
            vmem((2, CHUNKS, 2, HALF, 256), BF16),
            vmem((2, Q * HALF, 256), BF16),
            vmem((4 * BEAMS, 128), F32),
            dma((COLS,)),
            dma((COLS,)),
            dma((COLS,)),
            dma((COLS,)),
            dma((CHUNKS, COLS)),
            dma((CHUNKS, COLS)),
            dma((3, ROWS)),
            dma((3, ROWS)),
            dma((2, CHUNKS)),
            dma((2, CHUNKS)),
        ],
        compiler_params=pltpu.CompilerParams(
            collective_id=0, has_side_effects=True, vmem_limit_bytes=40 << 20
        ),
        name="backprojection",
    )(
        raw_samples,
        window.reshape(1, NS),
        steering.reshape(2 * P_DEV, BEAMS),
        assignment.reshape(1, P_DEV),
        beam_map.reshape(4, BEAMS),
        interp_index.reshape(4, BEAMS),
        phase_offset.reshape(4, BEAMS),
        phase_rate.reshape(4, BEAMS),
        interp_bank.reshape(Q * RT, RT),
    )
    out = out.reshape(BEAMS, CHUNKS, 2, RT).transpose(0, 2, 1, 3)
    return out.reshape(1, 1, BEAMS, 2, CHUNKS * RT)


def solution(mesh):
    in_specs = (
        P(None, ("grp", "row", "col"), None),
        P(),
        P(("grp", "row", "col"), None, None),
        P(("grp", "row", "col"), None),
        P(None, "grp", "row", None, None),
        P(None, "grp", "row", None, None),
        P(None, "grp", "row", None, None),
        P(None, "grp", "row", None, None),
        P(),
    )
    out_specs = P("grp", "row", None, None, "col")
    return jax.shard_map(body, mesh=mesh, in_specs=in_specs, out_specs=out_specs, check_vma=False)
```

time: 199 us -> 44 us (0.22)
  other arithmetic: 109 us -> 0 us
  Pallas kernels: 0 us -> 39 us
  starting transfers between devices: 33.4 us -> 0 us
  waiting for transfers between devices: 25.3 us -> 0 us
  local copies, waits for them, and re-layouts: 24.8 us -> 4.67 us
  matrix products: 5.37 us -> 0 us
    convert_element_type x3 -> x0, other arithmetic: 69.7 us -> none  [the longest x1 68.2 us: spectral_tables(): cos_table = (jnp.cos(phase_angle) * scaling).astype(jnp.bfloat16)]
    pallas_call x0 -> x1, Pallas kernels: none -> 39 us  [body(): pl.pallas_call(kernel, out_shape=jax.ShapeDtypeStruct((4 * BEAMS, 128), B...]
    all_to_all x2 -> x0, starting transfers between devices: 29.8 us -> none  [the longest x1 16.3 us: body(): lax.all_to_all(weight_buffer.reshape(row_count * col_count, capacity, 2,...]
    all_to_all x2 -> x0, waiting for transfers between devices: 21.3 us -> none  [the longest x1 21.3 us: body(): lax.all_to_all(data_buffer.reshape(row_count * col_count, capacity, 2, ra...]
    select_n x13 -> x0, other arithmetic: 15.7 us -> none  [the longest x4 11.4 us: interpolate(): jnp.where((quants == bank_index)[:, None, None, None], all_phases[:, :, :...]
    squeeze x32 -> x0, local copies, waits for them, and re-layouts: 11.7 us -> none  [the longest x28 9.68 us: interpolate(): all_phases[:, :, :, bank_index]]
    another operation x5 -> x0, other arithmetic: 9.9 us -> none  [the longest x1 9.75 us: interpolate(): return jnp.stack([real_part, imag_part], axis=1)]
    sub x1 -> x0, other arithmetic: 9.01 us -> none  [interpolate(): real_part = chosen[:, 0] * cosine - chosen[:, 1] * sine_part]
  transfers between devices with their start and end apart: 4 -> 0, of which waited for: 3 -> 0; matrix products, arithmetic and copies ran while one was open for 41% -> 0% of each run, Pallas kernels for 0% -> 0%
where the time goes in v1:
time: 44 us; the launch traced here: 43.7 us
  Pallas kernels  39 us (89%)
  local copies, waits for them, and re-layouts  4.67 us (11%)
    pallas_call x1, Pallas kernels, body(): pl.pallas_call(kernel, out_shape=jax.ShapeDtypeStruct((4 * BEAMS, 128), B...  39 us
    unnamed x19, local copies, waits for them, and re-layouts  4.67 us

profile of v1, /device:TPU:1, one launch (start us, length us, event | category | flops | bytes accessed | tf_op | source)
XLA Modules:
  0.0 43.7 jit_solution(9534232825821831667)
XLA Ops:
  0.0 0.0 copy-start.3
  0.0 0.0 copy-start.6
  0.0 0.0 copy-start.5
  0.0 0.0 copy-start.4
  0.0 0.0 copy-start.8
  0.0 0.7 %copy-done.3 = f32[2048]{0:T(1024)S(1)} copy-done((f32[2048]{0:T(1024)S(1)}, f32[2048]{0:T(1024)}, u32[]{:S(2)}) %copy-start.3) | copy-done | bytes 8216
  0.7 0.0 copy-done.6
  0.7 0.0 copy-done.5
  0.7 0.0 copy-done.4
  0.7 0.0 copy-done.8
  0.7 0.0 copy-start
  0.7 0.9 %copy-done = bf16[2,32,2048]{2,1,0:T(8,128)(2,1)S(1)} copy-done((bf16[2,32,2048]{2,1,0:T(8,128)(2,1)S(1)}, bf16[2,32,2048]{2,1,0:T(8,128)(2,1)}, u32[]{:S(2)}) %copy-start) | copy-done | bytes 262168
  1.7 0.0 copy-start.1
  1.7 0.9 %copy-done.1 = bf16[8,128,128]{2,1,0:T(8,128)(2,1)S(1)} copy-done((bf16[8,128,128]{2,1,0:T(8,128)(2,1)S(1)}, bf16[8,128,128]{2,1,0:T(8,128)(2,1)}, u32[]{:S(2)}) %copy-start.1) | copy-done | bytes 262168
  2.6 0.0 copy-start.2
  2.6 0.7 %copy-done.2 = bf16[32,2,128]{2,1,0:T(2,128)(2,1)S(1)} copy-done((bf16[32,2,128]{2,1,0:T(2,128)(2,1)S(1)}, bf16[32,2,128]{2,1,0:T(2,128)(2,1)}, u32[]{:S(2)}) %copy-start.2) | copy-done | bytes 16408
  3.4 0.0 copy-start.7
  3.4 0.7 %copy-done.7 = f32[2,1,1,2,128]{4,3,2,1,0:T(2,128)S(1)} copy-done((f32[2,1,1,2,128]{4,3,2,1,0:T(2,128)S(1)}, f32[2,1,1,2,128]{4,3,2,1,0:T(2,128)}, u32[]{:S(2)}) %copy-start.7) | copy-done | bytes 2072
  4.0 39.0 %backprojection.1 = bf16[512,128]{1,0:T(8,128)(2,1)S(1)} custom-call(bf16[2,32,2048]{2,1,0:T(8,128)(2,1)S(1)} %copy-done, f32[1,2048]{1,0:T(1,128)S(1)} %bitcast.16, bf16[64,128]{1,0:T(8,128)(2,1)S(1)} %bitcast.15, s32[1,32]{1,0:T(1,128)S(1)} %bitcast.21, s32[4,128]{1,0:T(4,128)S(1)} %bitcast.17, s32[4,128]{1,0:T(4,128)S(1)} %bitcast.18, ...), custom_call_target="tpu_custom_call" | custom-call | tf_op jit(solution)/shard_map/backprojection/pallas_call | solution.py:461
  43.1 0.7 %copy.12 = bf16[1,1,128,2,256]{4,3,2,1,0:T(2,128)(2,1)} copy(bf16[1,1,128,2,256]{4,3,2,1,0:T(2,128)(2,1)S(1)} %bitcast.13) | data formatting | bytes 262144
Async XLA Ops:
  0.0 0.7 %copy-start.3 = (f32[2048]{0:T(1024)S(1)}, f32[2048]{0:T(1024)}, u32[]{:S(2)}) copy-start(f32[2048]{0:T(1024)} %param.10) | copy-start | bytes 24580
  0.0 0.7 %copy-start.6 = (f32[2,1,1,2,128]{4,3,2,1,0:T(2,128)S(1)}, f32[2,1,1,2,128]{4,3,2,1,0:T(2,128)}, u32[]{:S(2)}) copy-start(f32[2,1,1,2,128]{4,3,2,1,0:T(2,128)} %param.15) | copy-start | bytes 6148
  0.0 0.7 %copy-start.5 = (s32[2,1,1,2,128]{4,3,2,1,0:T(2,128)S(1)}, s32[2,1,1,2,128]{4,3,2,1,0:T(2,128)}, u32[]{:S(2)}) copy-start(s32[2,1,1,2,128]{4,3,2,1,0:T(2,128)} %param.14) | copy-start | bytes 6148
  0.0 0.7 %copy-start.4 = (s32[2,1,1,2,128]{4,3,2,1,0:T(2,128)S(1)}, s32[2,1,1,2,128]{4,3,2,1,0:T(2,128)}, u32[]{:S(2)}) copy-start(s32[2,1,1,2,128]{4,3,2,1,0:T(2,128)} %param.13) | copy-start | bytes 6148
  0.0 0.7 %copy-start.8 = (s32[32,1]{0,1:T(1,128)S(1)}, s32[32,1]{0,1:T(1,128)}, u32[]{:S(2)}) copy-start(s32[32,1]{0,1:T(1,128)} %param.12) | copy-start | bytes 388
  0.7 1.0 %copy-start = (bf16[2,32,2048]{2,1,0:T(8,128)(2,1)S(1)}, bf16[2,32,2048]{2,1,0:T(8,128)(2,1)}, u32[]{:S(2)}) copy-start(bf16[2,32,2048]{2,1,0:T(8,128)(2,1)} %raw.1) | copy-start | bytes 786436
  1.7 0.9 %copy-start.1 = (bf16[8,128,128]{2,1,0:T(8,128)(2,1)S(1)}, bf16[8,128,128]{2,1,0:T(8,128)(2,1)}, u32[]{:S(2)}) copy-start(bf16[8,128,128]{2,1,0:T(8,128)(2,1)} %param.17) | copy-start | bytes 786436
  2.6 0.7 %copy-start.2 = (bf16[32,2,128]{2,1,0:T(2,128)(2,1)S(1)}, bf16[32,2,128]{2,1,0:T(2,128)(2,1)}, u32[]{:S(2)}) copy-start(bf16[32,2,128]{2,1,0:T(2,128)(2,1)} %param.11) | copy-start | bytes 49156
  3.4 0.7 %copy-start.7 = (f32[2,1,1,2,128]{4,3,2,1,0:T(2,128)S(1)}, f32[2,1,1,2,128]{4,3,2,1,0:T(2,128)}, u32[]{:S(2)}) copy-start(f32[2,1,1,2,128]{4,3,2,1,0:T(2,128)} %param.16) | copy-start | bytes 6148

commit v2 on v1

--- a/solution.py
+++ b/solution.py
@@ -100,6 +100,16 @@
 
 
 def kernel(
+    raw_in,
+    window_in,
+    steering_in,
+    assignment_in,
+    beam_map_in,
+    interp_index_in,
+    phase_offset_in,
+    phase_rate_in,
+    bank_in,
+    out,
     raw,
     window,
     steering,
@@ -109,7 +119,6 @@
     phase_offset,
     phase_rate,
     bank,
-    out,
     ybuf,
     table,
     twiddle,
@@ -122,6 +131,8 @@
     sel,
     slots,
     got,
+    w_slots,
+    w_got,
     weights_t,
     par,
     bank_nat,
@@ -133,6 +144,7 @@
     child,
     vbuf,
     outf,
+    in_sems,
     st_send,
     st_recv,
     code_send,
@@ -141,6 +153,8 @@
     z_recv,
     r_send,
     r_recv,
+    p_send,
+    p_recv,
     x_send,
     x_recv,
 ):
@@ -157,6 +171,25 @@
             device_id_type=MESH,
         )
 
+    loads = [
+        pltpu.make_async_copy(src, dst, in_sems.at[i])
+        for i, (src, dst) in enumerate(
+            (
+                (assignment_in, assignment),
+                (steering_in, steering),
+                (window_in, window),
+                (raw_in, raw),
+                (beam_map_in, beam_map),
+                (interp_index_in, interp_index),
+                (phase_offset_in, phase_offset),
+                (phase_rate_in, phase_rate),
+                (bank_in, bank),
+            )
+        )
+    ]
+    for load in loads:
+        load.start()
+
     barrier = pltpu.get_barrier_semaphore()
 
     def greet_col(i, _):
@@ -175,6 +208,7 @@
     lax.fori_loop(1, ROWS, greet_row, 0)
     pl.semaphore_signal(barrier, inc=1, device_id=(1 - g, row, col), device_id_type=MESH)
 
+    loads[0].wait()
     own_row = assignment[...].astype(F32)
     eye = iota((P_DEV, P_DEV), 0) == iota((P_DEV, P_DEV), 1)
     before = iota((P_DEV, P_DEV), 1) < iota((P_DEV, P_DEV), 0)
@@ -187,28 +221,30 @@
     code = jnp.sum(
         jnp.where(iota((P_DEV, 128), 1) == place, code_col, 0.0), axis=0, keepdims=True
     )
-    code_own[...] = jnp.broadcast_to(code, (8, 128))
-
+    code_own[...] = code
+
+    loads[1].wait()
     pick = iota((2 * P_DEV, 2 * P_DEV), 0)
     pick = (pick % P_DEV) * 2 + pick // P_DEV == iota((2 * P_DEV, 2 * P_DEV), 1)
     parts = dot(pick.astype(F32).astype(BF16), steering[...]).astype(BF16)
-    st_own[:, :BEAMS] = parts[:P_DEV]
-    st_own[:, BEAMS:] = parts[P_DEV:]
+    st_own[0] = parts[:P_DEV]
+    st_own[1] = parts[P_DEV:]
 
     pl.semaphore_wait(barrier, COLS - 1 + ROWS - 1 + 1)
 
+    parity = col % 2
     first_sends = []
     for i in range(1, COLS):
         dest = (col + i) % COLS
         device = (g, row, dest)
         mine = pl.ds(pl.multiple_of(col * P_DEV, P_DEV), P_DEV)
         c1 = remote(code_own, code_all.at[col], code_send.at[i], code_recv.at[col], device)
-        c2 = remote(st_own, st_all.at[mine], st_send.at[i], st_recv.at[col], device)
+        c2 = remote(st_own.at[dest % 2], st_all.at[mine], st_send.at[i], st_recv.at[col], device)
         c1.start()
         c2.start()
         first_sends += [c1, c2]
     code_all[col] = code_own[...]
-    st_all[pl.ds(pl.multiple_of(col * P_DEV, P_DEV), P_DEV), :] = st_own[...]
+    st_all[pl.ds(pl.multiple_of(col * P_DEV, P_DEV), P_DEV), :] = st_own[parity]
 
     steps = (iota((8, 256), 0) * iota((8, 256), 1)).astype(F32) * (1.0 / NS)
     tc, ts = cos_sin(steps)
@@ -225,6 +261,8 @@
         table[m, 256:, :128] = s
         table[m, 256:, 128:] = c
 
+    loads[2].wait()
+    loads[3].wait()
     scale = 1.0 / math.sqrt(NS)
     for lh in range(2):
         lanes = [pl.ds(256 * t + 128 * lh, 128) for t in range(8)]
@@ -280,13 +318,13 @@
             code_own, code_all.at[source], code_send.at[0], code_recv.at[source], (g, row, source)
         ).wait_recv()
         remote(
-            st_own, st_all.at[at], st_send.at[0], st_recv.at[source], (g, row, source)
+            st_own.at[0], st_all.at[at], st_send.at[0], st_recv.at[source], (g, row, source)
         ).wait_recv()
 
     from_cols(wait_first)
     low = code_all[0] + code_all[1] + code_all[2] + code_all[3]
     high = code_all[4] + code_all[5] + code_all[6] + code_all[7]
-    codes = jnp.concatenate([low[:1], high[:1]], axis=1).astype(I32)
+    codes = jnp.concatenate([low, high], axis=1).astype(I32)
     for y in range(4):
         sel[192 * y : 192 * y + 192] = jnp.where(
             iota((192, 256), 0) + 192 * y == codes, 1.0, 0.0
@@ -294,21 +332,21 @@
 
     row_sends = []
 
-    def to_owners(kind, data):
+    def to_owners(kind, data, packed, landed):
         mine = pl.ds(pl.multiple_of(row * SLOTS, SLOTS), SLOTS)
         for dy in (2, 1, 3, 0):
             y = (ry + dy) % 4
             block = pl.ds(pl.multiple_of(y * 4 * SLOTS, 4 * SLOTS), 4 * SLOTS)
-            slots[kind, block, :] = dot(sel[block, :], data[...]).astype(BF16)
+            packed[block, :] = dot(sel[block, :], data[...]).astype(BF16)
             for dx in (2, 1, 3, 0):
                 dest = y * 4 + (rx + dx) % 4
                 there = pl.ds(pl.multiple_of(dest * SLOTS, SLOTS), SLOTS)
                 if dy == 0 and dx == 0:
-                    got[kind, mine, :] = slots[kind, mine, :]
+                    landed[mine, :] = packed[mine, :]
                     continue
                 c1 = remote(
-                    slots.at[kind, there],
-                    got.at[kind, mine],
+                    packed.at[there],
+                    landed.at[mine],
                     r_send.at[kind, 4 * dy + dx],
                     r_recv.at[kind, row],
                     (g, dest, col),
@@ -316,19 +354,33 @@
                 c1.start()
                 row_sends.append(c1)
 
-    def from_rows(kind):
-        for i in range(1, ROWS):
-            source = (row + i) % ROWS
-            at = pl.ds(pl.multiple_of(source * SLOTS, SLOTS), SLOTS)
-            remote(
-                slots.at[kind, at],
-                got.at[kind, at],
-                r_send.at[kind, 0],
-                r_recv.at[kind, source],
-                (g, source, col),
-            ).wait_recv()
-
-    to_owners(2, st_all)
+    def from_rows(kind, packed, landed, dys=(2, 1, 3, 0)):
+        for dy in dys:
+            for dx in (2, 1, 3, 0):
+                if dy == 0 and dx == 0:
+                    continue
+                source = (ry - dy + 4) % 4 * 4 + (rx - dx + 4) % 4
+                at = pl.ds(pl.multiple_of(source * SLOTS, SLOTS), SLOTS)
+                remote(
+                    packed.at[at],
+                    landed.at[at],
+                    r_send.at[kind, 0],
+                    r_recv.at[kind, source],
+                    (g, source, col),
+                ).wait_recv()
+
+    def col_pass(i, part):
+        y = (ry - i + 4) % 4
+        block = pl.ds(pl.multiple_of(y * 4 * SLOTS, 4 * SLOTS), 4 * SLOTS)
+        return remote(
+            w_got.at[part, block],
+            w_got.at[part, block],
+            p_send.at[i],
+            p_recv.at[i],
+            (g, row, col + 1 - 2 * parity),
+        )
+
+    to_owners(2, st_all, w_slots, w_got.at[parity])
 
     for m in range(CHUNKS):
 
@@ -343,8 +395,16 @@
             ).wait_recv()
 
         from_cols(wait_z)
-        to_owners(m, zall.at[m])
-
+        to_owners(m, zall.at[m], slots.at[m], got.at[m])
+        if m == 0:
+            for dy in (2, 1, 3, 0):
+                from_rows(2, w_slots, w_got.at[parity], (dy,))
+                c1 = col_pass(dy, parity)
+                c1.start()
+                row_sends.append(c1)
+
+    for load in loads[4:]:
+        load.wait()
     par[...] = jnp.zeros_like(par)
     par[0:4, :] = (interp_index[...] * HALF + beam_map[...]).astype(F32)
     par[8:12, :] = phase_offset[...]
@@ -364,8 +424,10 @@
     order = ((lane % 16) * 8 + lane // 16 == iota((RT, RT), 1)).astype(F32).astype(BF16)
     bank_perm[...] = dot(order, bank_nat[...]).astype(BF16)
 
-    from_rows(2)
-    weights_t[...] = got[2].T
+    for dy in (2, 1, 3, 0):
+        col_pass(dy, 1 - parity).wait_recv()
+    weights_t[:BEAMS] = w_got[0].T
+    weights_t[BEAMS:] = w_got[1].T
 
     def merge(level, m, matrices):
         lhs = jnp.concatenate(
@@ -419,7 +481,7 @@
     partner = (g, row + 1 - 2 * v, col)
     x_sends = []
     for m in range(CHUNKS):
-        from_rows(m)
+        from_rows(m, slots.at[m], got.at[m])
         a = dot(weights_t[...], got[m])
         x_sends.append(
             exchange(
@@ -461,21 +523,32 @@
     out = pl.pallas_call(
         kernel,
         out_shape=jax.ShapeDtypeStruct((4 * BEAMS, 128), BF16),
-        in_specs=[pl.BlockSpec(memory_space=pltpu.VMEM)] * 9,
+        in_specs=[pl.BlockSpec(memory_space=pltpu.HBM)] * 9,
         out_specs=pl.BlockSpec(memory_space=pltpu.VMEM),
         scratch_shapes=[
+            vmem((2, P_DEV, NS), BF16),
+            vmem((1, NS), F32),
+            vmem((2 * P_DEV, BEAMS), BF16),
+            vmem((1, P_DEV), I32),
+            vmem((4, BEAMS), I32),
+            vmem((4, BEAMS), I32),
+            vmem((4, BEAMS), F32),
+            vmem((4, BEAMS), F32),
+            vmem((Q * RT, RT), BF16),
             vmem((8 * P_DEV, 512), BF16),
             vmem((CHUNKS, 512, 256), BF16),
             vmem((2, 8, 256), F32),
-            vmem((P_DEV, 256), BF16),
-            vmem((COLS * P_DEV, 256), BF16),
-            vmem((8, 128), F32),
-            vmem((COLS, 8, 128), F32),
+            vmem((2, P_DEV, BEAMS), BF16),
+            vmem((COLS * P_DEV, BEAMS), BF16),
+            vmem((1, 128), F32),
+            vmem((COLS, 1, 128), F32),
             vmem((CHUNKS, COLS, P_DEV, 256), BF16),
             vmem((CHUNKS, COLS * P_DEV, 256), BF16),
             vmem((ROWS * SLOTS, 256), BF16),
-            vmem((3, ROWS * SLOTS, 256), BF16),
-            vmem((3, ROWS * SLOTS, 256), BF16),
+            vmem((CHUNKS, ROWS * SLOTS, 256), BF16),
+            vmem((CHUNKS, ROWS * SLOTS, 256), BF16),
+            vmem((ROWS * SLOTS, BEAMS), BF16),
+            vmem((2, ROWS * SLOTS, BEAMS), BF16),
             vmem((256, ROWS * SLOTS), BF16),
             vmem((128, 128), F32),
             vmem((RT, Q * RT), BF16),
@@ -487,6 +560,7 @@
             vmem((2, CHUNKS, 2, HALF, 256), BF16),
             vmem((2, Q * HALF, 256), BF16),
             vmem((4 * BEAMS, 128), F32),
+            dma((9,)),
             dma((COLS,)),
             dma((COLS,)),
             dma((COLS,)),
@@ -495,11 +569,13 @@
             dma((CHUNKS, COLS)),
             dma((3, ROWS)),
             dma((3, ROWS)),
+            dma((4,)),
+            dma((4,)),
             dma((2, CHUNKS)),
             dma((2, CHUNKS)),
         ],
         compiler_params=pltpu.CompilerParams(
-            collective_id=0, has_side_effects=True, vmem_limit_bytes=40 << 20
+            collective_id=0, has_side_effects=True, vmem_limit_bytes=56 << 20
         ),
         name="backprojection",
     )(

time: 44 us -> 38.3 us (0.87)
  local copies, waits for them, and re-layouts: 4.67 us -> 1.65 us
  Pallas kernels: 39 us -> 36.6 us
    unnamed x19 -> x1, local copies, waits for them, and re-layouts: 4.67 us -> 1.65 us
    pallas_call x1, Pallas kernels: 39 us -> 36.6 us  [body(): pl.pallas_call(kernel, out_shape=jax.ShapeDtypeStruct((4 * BEAMS, 128), B...]
where the time goes in v2:
time: 38.3 us; the launch traced here: 38.2 us
  Pallas kernels  36.6 us (96%)
  local copies, waits for them, and re-layouts  1.65 us (4%)
    pallas_call x1, Pallas kernels, body(): pl.pallas_call(kernel, out_shape=jax.ShapeDtypeStruct((4 * BEAMS, 128), B...  36.6 us
    unnamed x1, local copies, waits for them, and re-layouts  1.65 us

profile of v2, /device:TPU:1, one launch (start us, length us, event | category | flops | bytes accessed | tf_op | source)
XLA Modules:
  0.0 38.2 jit_solution(7350358139154079492)
XLA Ops:
  0.0 36.6 %backprojection.1 = bf16[512,128]{1,0:T(8,128)(2,1)} custom-call(bf16[2,32,2048]{2,1,0:T(8,128)(2,1)} %raw_in.1, f32[1,2048]{1,0:T(1,128)} %bitcast.16, bf16[64,128]{1,0:T(8,128)(2,1)} %bitcast.15, s32[1,32]{1,0:T(1,128)} %bitcast.21, s32[4,128]{1,0:T(4,128)} %bitcast.17, s32[4,128]{1,0:T(4,128)} %bitcast.18, f32[4,128]{1,0:T(4,128)} %bitcast.19, ...), custom_call_target="tpu_custom_call" | custom-call | tf_op jit(solution)/shard_map/backprojection/pallas_call | solution.py:523
  36.6 1.7 %copy.12 = bf16[1,1,128,2,256]{4,3,2,1,0:T(2,128)(2,1)} copy(bf16[1,1,128,2,256]{4,3,2,1,0:T(2,128)(2,1)} %bitcast.13) | data formatting | bytes 262144

commit v3 on v2

--- a/solution.py
+++ b/solution.py
@@ -208,6 +208,21 @@
     lax.fori_loop(1, ROWS, greet_row, 0)
     pl.semaphore_signal(barrier, inc=1, device_id=(1 - g, row, col), device_id_type=MESH)
 
+    steps = (iota((8, 256), 0) * iota((8, 256), 1)).astype(F32) * (1.0 / NS)
+    tc, ts = cos_sin(steps)
+    twiddle[0] = tc
+    twiddle[1] = ts
+    for m in range(CHUNKS):
+        lane = iota((256, 128), 1)
+        d = (lane // 16) * 32 + 16 * m + lane % 16
+        turns = ((iota((256, 128), 0) * d) % 256).astype(F32) * (1.0 / 256)
+        c, s = cos_sin(turns)
+        c, s = c.astype(BF16), s.astype(BF16)
+        table[m, :256, :128] = c
+        table[m, :256, 128:] = -s
+        table[m, 256:, :128] = s
+        table[m, 256:, 128:] = c
+
     loads[0].wait()
     own_row = assignment[...].astype(F32)
     eye = iota((P_DEV, P_DEV), 0) == iota((P_DEV, P_DEV), 1)
@@ -245,21 +260,6 @@
         first_sends += [c1, c2]
     code_all[col] = code_own[...]
     st_all[pl.ds(pl.multiple_of(col * P_DEV, P_DEV), P_DEV), :] = st_own[parity]
-
-    steps = (iota((8, 256), 0) * iota((8, 256), 1)).astype(F32) * (1.0 / NS)
-    tc, ts = cos_sin(steps)
-    twiddle[0] = tc
-    twiddle[1] = ts
-    for m in range(CHUNKS):
-        lane = iota((256, 128), 1)
-        d = (lane // 16) * 32 + 16 * m + lane % 16
-        turns = ((iota((256, 128), 0) * d) % 256).astype(F32) * (1.0 / 256)
-        c, s = cos_sin(turns)
-        c, s = c.astype(BF16), s.astype(BF16)
-        table[m, :256, :128] = c
-        table[m, :256, 128:] = -s
-        table[m, 256:, :128] = s
-        table[m, 256:, 128:] = c
 
     loads[2].wait()
     loads[3].wait()
@@ -294,8 +294,10 @@
             )
             for c in range(8):
                 dsend[m, c, :, 128 * part : 128 * part + 128] = tiles[c].astype(BF16)
+
+    def to_cols(m):
         mine = pl.ds(pl.multiple_of(col * P_DEV, P_DEV), P_DEV)
-        for i in range(1, COLS):
+        for i in (4, 3, 5, 2, 6, 1, 7):
             dest = (col + i) % COLS
             c1 = remote(
                 dsend.at[m, dest],
@@ -307,6 +309,8 @@
             c1.start()
             z_sends.append(c1)
         zall[m, mine, :] = dsend[m, col]
+
+    to_cols(0)
 
     def from_cols(wait):
         for i in range(1, COLS):
@@ -381,6 +385,7 @@
         )
 
     to_owners(2, st_all, w_slots, w_got.at[parity])
+    to_cols(1)
 
     for m in range(CHUNKS):
 
@@ -522,7 +527,7 @@
     vmem = pltpu.VMEM
     out = pl.pallas_call(
         kernel,
-        out_shape=jax.ShapeDtypeStruct((4 * BEAMS, 128), BF16),
+        out_shape=pltpu.VMEM((4 * BEAMS, 128), BF16),
         in_specs=[pl.BlockSpec(memory_space=pltpu.HBM)] * 9,
         out_specs=pl.BlockSpec(memory_space=pltpu.VMEM),
         scratch_shapes=[

time: 38.3 us -> 35.7 us (0.932)
  Pallas kernels: 36.6 us -> 34.9 us
  local copies, waits for them, and re-layouts: 1.65 us -> 0.66 us
    pallas_call x1, Pallas kernels: 36.6 us -> 34.9 us  [body(): pl.pallas_call(kernel, out_shape=pltpu.VMEM((4 * BEAMS, 128), BF16), in_s...]
    unnamed x1, local copies, waits for them, and re-layouts: 1.65 us -> 0.66 us
where the time goes in v3:
time: 35.7 us; the launch traced here: 35.6 us
  Pallas kernels  34.9 us (98%)
  local copies, waits for them, and re-layouts  0.66 us (2%)
    pallas_call x1, Pallas kernels, body(): pl.pallas_call(kernel, out_shape=pltpu.VMEM((4 * BEAMS, 128), BF16), in_s...  34.9 us

profile of v3, /device:TPU:1, one launch (start us, length us, event | category | flops | bytes accessed | tf_op | source)
XLA Modules:
  0.0 35.6 jit_solution(15282727788749650181)
XLA Ops:
  0.0 34.9 %backprojection.1 = bf16[512,128]{1,0:T(8,128)(2,1)S(1)} custom-call(bf16[2,32,2048]{2,1,0:T(8,128)(2,1)} %raw_in.1, f32[1,2048]{1,0:T(1,128)} %bitcast.16, bf16[64,128]{1,0:T(8,128)(2,1)} %bitcast.15, s32[1,32]{1,0:T(1,128)} %bitcast.21, s32[4,128]{1,0:T(4,128)} %bitcast.17, s32[4,128]{1,0:T(4,128)} %bitcast.18, f32[4,128]{1,0:T(4,128)} %bitcast.19, ...), custom_call_target="tpu_custom_call" | custom-call | tf_op jit(solution)/shard_map/backprojection/pallas_call | solution.py:528
  34.9 0.7 %copy.12 = bf16[1,1,128,2,256]{4,3,2,1,0:T(2,128)(2,1)} copy(bf16[1,1,128,2,256]{4,3,2,1,0:T(2,128)(2,1)S(1)} %bitcast.13) | data formatting | bytes 262144

commit v4 on v3

--- a/solution.py
+++ b/solution.py
@@ -77,11 +77,11 @@
 
 
 def swap_groups(tiles):
-    group = lax.broadcasted_iota(I32, tiles[0].shape, 1) // 16
+    lane = lax.broadcasted_iota(I32, tiles[0].shape, 1)
     tiles = list(tiles)
     for bit in range(3):
         step = 1 << bit
-        upper = (group // step) % 2 == 1
+        upper = (lane & (16 * step)) != 0
         for a in range(8):
             if a & step:
                 continue
@@ -212,11 +212,11 @@
     tc, ts = cos_sin(steps)
     twiddle[0] = tc
     twiddle[1] = ts
+    sample = iota((256, 128), 0).astype(F32)
+    lane = iota((1, 128), 1)
     for m in range(CHUNKS):
-        lane = iota((256, 128), 1)
-        d = (lane // 16) * 32 + 16 * m + lane % 16
-        turns = ((iota((256, 128), 0) * d) % 256).astype(F32) * (1.0 / 256)
-        c, s = cos_sin(turns)
+        d = ((lane >> 4) * 32 + (16 * m) + (lane & 15)).astype(F32) * (1.0 / 256)
+        c, s = cos_sin(sample * d)
         c, s = c.astype(BF16), s.astype(BF16)
         table[m, :256, :128] = c
         table[m, :256, 128:] = -s
@@ -249,7 +249,7 @@
 
     parity = col % 2
     first_sends = []
-    for i in range(1, COLS):
+    for i in (4, 3, 5, 2, 6, 1, 7):
         dest = (col + i) % COLS
         device = (g, row, dest)
         mine = pl.ds(pl.multiple_of(col * P_DEV, P_DEV), P_DEV)
@@ -297,7 +297,7 @@
 
     def to_cols(m):
         mine = pl.ds(pl.multiple_of(col * P_DEV, P_DEV), P_DEV)
-        for i in (4, 3, 5, 2, 6, 1, 7):
+        for i in (1, 4, 7, 3, 5, 2, 6):
             dest = (col + i) % COLS
             c1 = remote(
                 dsend.at[m, dest],
@@ -311,6 +311,7 @@
         zall[m, mine, :] = dsend[m, col]
 
     to_cols(0)
+    to_cols(1)
 
     def from_cols(wait):
         for i in range(1, COLS):
@@ -342,7 +343,7 @@
             y = (ry + dy) % 4
             block = pl.ds(pl.multiple_of(y * 4 * SLOTS, 4 * SLOTS), 4 * SLOTS)
             packed[block, :] = dot(sel[block, :], data[...]).astype(BF16)
-            for dx in (2, 1, 3, 0):
+            for dx in (0, 2, 1, 3):
                 dest = y * 4 + (rx + dx) % 4
                 there = pl.ds(pl.multiple_of(dest * SLOTS, SLOTS), SLOTS)
                 if dy == 0 and dx == 0:
@@ -360,7 +361,7 @@
 
     def from_rows(kind, packed, landed, dys=(2, 1, 3, 0)):
         for dy in dys:
-            for dx in (2, 1, 3, 0):
+            for dx in (0, 2, 1, 3):
                 if dy == 0 and dx == 0:
                     continue
                 source = (ry - dy + 4) % 4 * 4 + (rx - dx + 4) % 4
@@ -385,7 +386,6 @@
         )
 
     to_owners(2, st_all, w_slots, w_got.at[parity])
-    to_cols(1)
 
     for m in range(CHUNKS):
 
@@ -401,12 +401,12 @@
 
         from_cols(wait_z)
         to_owners(m, zall.at[m], slots.at[m], got.at[m])
-        if m == 0:
-            for dy in (2, 1, 3, 0):
-                from_rows(2, w_slots, w_got.at[parity], (dy,))
-                c1 = col_pass(dy, parity)
-                c1.start()
-                row_sends.append(c1)
+
+    for dy in (2, 1, 3, 0):
+        from_rows(2, w_slots, w_got.at[parity], (dy,))
+        c1 = col_pass(dy, parity)
+        c1.start()
+        row_sends.append(c1)
 
     for load in loads[4:]:
         load.wait()
@@ -434,78 +434,86 @@
     weights_t[:BEAMS] = w_got[0].T
     weights_t[BEAMS:] = w_got[1].T
 
-    def merge(level, m, matrices):
-        lhs = jnp.concatenate(
-            [child[level, m, s, :, 128 * part : 128 * part + 128] for s in range(2) for part in range(2)],
-            axis=0,
-        )
-        v = dot(lhs, matrices[...]).astype(BF16)
-        total = None
-        for s in range(2):
-            for part in range(2):
-                at = (2 * s + part) * HALF
-                for q in range(Q):
-                    vbuf[s, HALF * q : HALF * q + HALF, 128 * part : 128 * part + 128] = v[
-                        at : at + HALF, RT * q : RT * q + RT
-                    ]
-            t = dot(picks[2 * level + s], vbuf[s])
-            tr, ti = t[:, :128], t[:, 128:]
-            c = cosb[2 * level + s, :, 128 * m : 128 * m + 128]
-            d = sinb[2 * level + s, :, 128 * m : 128 * m + 128]
-            yr, yi = tr * c - ti * d, tr * d + ti * c
-            total = (yr, yi) if total is None else (total[0] + yr, total[1] + yi)
-        return total
-
-    def exchange(level, m, real, imag, bit, device):
+    def half(bit):
+        return pl.ds(pl.multiple_of(bit * HALF, HALF), HALF)
+
+    def interpolated(level, m, child_of, matrices, slot):
+        both = child[level, m, child_of]
+        v = dot(
+            jnp.concatenate([both[:, :128], both[:, 128:]], axis=0), matrices[...]
+        ).astype(BF16)
+        for part in range(2):
+            for q in range(Q):
+                vbuf[slot, HALF * q : HALF * q + HALF, 128 * part : 128 * part + 128] = v[
+                    HALF * part : HALF * part + HALF, RT * q : RT * q + RT
+                ]
+
+    def term(level, m, child_of, slot, beams):
+        t = dot(picks[2 * level + child_of, beams, :], vbuf[slot])
+        tr, ti = t[:, :128], t[:, 128:]
+        c = cosb[2 * level + child_of, beams, 128 * m : 128 * m + 128]
+        d = sinb[2 * level + child_of, beams, 128 * m : 128 * m + 128]
+        return tr * c - ti * d, tr * d + ti * c
+
+    def send(level, m, real, imag, bit, device):
         img[level, m, :, :128] = real.astype(BF16)
         img[level, m, :, 128:] = imag.astype(BF16)
-        keep = pl.ds(pl.multiple_of(bit * HALF, HALF), HALF)
-        give = pl.ds(pl.multiple_of((1 - bit) * HALF, HALF), HALF)
         c1 = remote(
-            img.at[level, m, give],
+            img.at[level, m],
             child.at[level, m, bit],
             x_send.at[level, m],
             x_recv.at[level, m],
             device,
         )
         c1.start()
-        child[level, m, bit] = img[level, m, keep, :]
-        return c1
+        x_sends.append(c1)
+
+    def keep(level, m, real, imag, bit):
+        child[level, m, bit, :, :128] = real.astype(BF16)
+        child[level, m, bit, :, 128:] = imag.astype(BF16)
 
     def arrive(level, m, bit, device):
         remote(
-            img.at[level, m, 0:HALF],
+            img.at[level, m],
             child.at[level, m, 1 - bit],
             x_send.at[level, m],
             x_recv.at[level, m],
             device,
         ).wait_recv()
 
+    def beams_of(m, bit):
+        lhs = jnp.concatenate(
+            [weights_t[half(bit), :], weights_t[half(bit + 2), :]], axis=0
+        )
+        a = dot(lhs, got[m])
+        return a[:HALF, :128] - a[HALF:, 128:], a[:HALF, 128:] + a[HALF:, :128]
+
     sibling = (1 - g, row, col)
     v = row % 2
     partner = (g, row + 1 - 2 * v, col)
+    every = slice(None)
     x_sends = []
     for m in range(CHUNKS):
         from_rows(m, slots.at[m], got.at[m])
-        a = dot(weights_t[...], got[m])
-        x_sends.append(
-            exchange(
-                0,
-                m,
-                a[:BEAMS, :128] - a[BEAMS:, 128:],
-                a[:BEAMS, 128:] + a[BEAMS:, :128],
-                g,
-                sibling,
-            )
-        )
+        send(0, m, *beams_of(m, 1 - g), g, sibling)
+        keep(0, m, *beams_of(m, g), g)
+        interpolated(0, m, g, bank_perm, 0)
+        give_r, give_i = term(0, m, g, 0, half(1 - v))
+        keep_r, keep_i = term(0, m, g, 0, half(v))
         arrive(0, m, g, sibling)
-        real, imag = merge(0, m, bank_perm)
-        x_sends.append(exchange(1, m, real, imag, v, partner))
+        interpolated(0, m, 1 - g, bank_perm, 1)
+        r, i = term(0, m, 1 - g, 1, half(1 - v))
+        send(1, m, give_r + r, give_i + i, v, partner)
+        r, i = term(0, m, 1 - g, 1, half(v))
+        keep(1, m, keep_r + r, keep_i + i, v)
     for m in range(CHUNKS):
+        interpolated(1, m, v, bank_nat, 0)
+        own_r, own_i = term(1, m, v, 0, every)
         arrive(1, m, v, partner)
-        real, imag = merge(1, m, bank_nat)
-        outf[pl.ds(2 * m, BEAMS, stride=4), :] = real
-        outf[pl.ds(2 * m + 1, BEAMS, stride=4), :] = imag
+        interpolated(1, m, 1 - v, bank_nat, 1)
+        r, i = term(1, m, 1 - v, 1, every)
+        outf[pl.ds(2 * m, BEAMS, stride=4), :] = own_r + r
+        outf[pl.ds(2 * m + 1, BEAMS, stride=4), :] = own_i + i
     out[...] = outf[...].astype(BF16)
 
     for c1 in first_sends + z_sends + row_sends + x_sends:
@@ -561,7 +569,7 @@
             vmem((4, BEAMS, Q * HALF), BF16),
             vmem((4, BEAMS, 256), F32),
             vmem((4, BEAMS, 256), F32),
-            vmem((2, CHUNKS, BEAMS, 256), BF16),
+            vmem((2, CHUNKS, HALF, 256), BF16),
             vmem((2, CHUNKS, 2, HALF, 256), BF16),
             vmem((2, Q * HALF, 256), BF16),
             vmem((4 * BEAMS, 128), F32),

time: 35.7 us -> 34.9 us (0.978)
  Pallas kernels: 34.9 us -> 34 us
    pallas_call x1, Pallas kernels: 34.9 us -> 34 us  [body(): pl.pallas_call(kernel, out_shape=pltpu.VMEM((4 * BEAMS, 128), BF16), in_s...]
where the time goes in v4:
time: 34.9 us; the launch traced here: 34.7 us
  Pallas kernels  34 us (97%)
  local copies, waits for them, and re-layouts  0.66 us (2%)
    pallas_call x1, Pallas kernels, body(): pl.pallas_call(kernel, out_shape=pltpu.VMEM((4 * BEAMS, 128), BF16), in_s...  34 us

profile of v4, /device:TPU:1, one launch (start us, length us, event | category | flops | bytes accessed | tf_op | source)
XLA Modules:
  0.0 34.7 jit_solution(3937294495807675227)
XLA Ops:
  0.0 34.0 %backprojection.1 = bf16[512,128]{1,0:T(8,128)(2,1)S(1)} custom-call(bf16[2,32,2048]{2,1,0:T(8,128)(2,1)} %raw_in.1, f32[1,2048]{1,0:T(1,128)} %bitcast.16, bf16[64,128]{1,0:T(8,128)(2,1)} %bitcast.15, s32[1,32]{1,0:T(1,128)} %bitcast.21, s32[4,128]{1,0:T(4,128)} %bitcast.17, s32[4,128]{1,0:T(4,128)} %bitcast.18, f32[4,128]{1,0:T(4,128)} %bitcast.19, ...), custom_call_target="tpu_custom_call" | custom-call | tf_op jit(solution)/shard_map/backprojection/pallas_call | solution.py:536
  34.1 0.7 %copy.12 = bf16[1,1,128,2,256]{4,3,2,1,0:T(2,128)(2,1)} copy(bf16[1,1,128,2,256]{4,3,2,1,0:T(2,128)(2,1)S(1)} %bitcast.13) | data formatting | bytes 262144

commit v5 on v4

--- a/solution.py
+++ b/solution.py
@@ -249,15 +249,21 @@
 
     parity = col % 2
     first_sends = []
+    mine = pl.ds(pl.multiple_of(col * P_DEV, P_DEV), P_DEV)
     for i in (4, 3, 5, 2, 6, 1, 7):
         dest = (col + i) % COLS
-        device = (g, row, dest)
-        mine = pl.ds(pl.multiple_of(col * P_DEV, P_DEV), P_DEV)
-        c1 = remote(code_own, code_all.at[col], code_send.at[i], code_recv.at[col], device)
-        c2 = remote(st_own.at[dest % 2], st_all.at[mine], st_send.at[i], st_recv.at[col], device)
+        c1 = remote(
+            code_own, code_all.at[col], code_send.at[i], code_recv.at[col], (g, row, dest)
+        )
         c1.start()
-        c2.start()
-        first_sends += [c1, c2]
+        first_sends.append(c1)
+    for i in (4, 3, 5, 2, 6, 1, 7):
+        dest = (col + i) % COLS
+        c1 = remote(
+            st_own.at[dest % 2], st_all.at[mine], st_send.at[i], st_recv.at[col], (g, row, dest)
+        )
+        c1.start()
+        first_sends.append(c1)
     code_all[col] = code_own[...]
     st_all[pl.ds(pl.multiple_of(col * P_DEV, P_DEV), P_DEV), :] = st_own[parity]
 
@@ -317,16 +323,18 @@
         for i in range(1, COLS):
             wait((col + i) % COLS)
 
-    def wait_first(source):
-        at = pl.ds(pl.multiple_of(source * P_DEV, P_DEV), P_DEV)
+    def wait_code(source):
         remote(
             code_own, code_all.at[source], code_send.at[0], code_recv.at[source], (g, row, source)
         ).wait_recv()
+
+    def wait_steering(source):
+        at = pl.ds(pl.multiple_of(source * P_DEV, P_DEV), P_DEV)
         remote(
             st_own.at[0], st_all.at[at], st_send.at[0], st_recv.at[source], (g, row, source)
         ).wait_recv()
 
-    from_cols(wait_first)
+    from_cols(wait_code)
     low = code_all[0] + code_all[1] + code_all[2] + code_all[3]
     high = code_all[4] + code_all[5] + code_all[6] + code_all[7]
     codes = jnp.concatenate([low, high], axis=1).astype(I32)
@@ -334,6 +342,7 @@
         sel[192 * y : 192 * y + 192] = jnp.where(
             iota((192, 256), 0) + 192 * y == codes, 1.0, 0.0
         ).astype(BF16)
+    from_cols(wait_steering)
 
     row_sends = []
 
@@ -429,10 +438,10 @@
     order = ((lane % 16) * 8 + lane // 16 == iota((RT, RT), 1)).astype(F32).astype(BF16)
     bank_perm[...] = dot(order, bank_nat[...]).astype(BF16)
 
+    weights_t[pl.ds(pl.multiple_of(parity * BEAMS, BEAMS), BEAMS), :] = w_got[parity].T
     for dy in (2, 1, 3, 0):
         col_pass(dy, 1 - parity).wait_recv()
-    weights_t[:BEAMS] = w_got[0].T
-    weights_t[BEAMS:] = w_got[1].T
+    weights_t[pl.ds(pl.multiple_of((1 - parity) * BEAMS, BEAMS), BEAMS), :] = w_got[1 - parity].T
 
     def half(bit):
         return pl.ds(pl.multiple_of(bit * HALF, HALF), HALF)

time: 34.9 us -> 34.8 us (level)
  no operation moved by 1% of the time
where the time goes in v5:
time: 34.8 us; the launch traced here: 34.7 us
  Pallas kernels  34 us (98%)
  local copies, waits for them, and re-layouts  0.66 us (2%)
    pallas_call x1, Pallas kernels, body(): pl.pallas_call(kernel, out_shape=pltpu.VMEM((4 * BEAMS, 128), BF16), in_s...  34 us

profile of v5, /device:TPU:1, one launch (start us, length us, event | category | flops | bytes accessed | tf_op | source)
XLA Modules:
  0.0 34.7 jit_solution(14392028043466418053)
XLA Ops:
  0.0 34.0 %backprojection.1 = bf16[512,128]{1,0:T(8,128)(2,1)S(1)} custom-call(bf16[2,32,2048]{2,1,0:T(8,128)(2,1)} %raw_in.1, f32[1,2048]{1,0:T(1,128)} %bitcast.16, bf16[64,128]{1,0:T(8,128)(2,1)} %bitcast.15, s32[1,32]{1,0:T(1,128)} %bitcast.21, s32[4,128]{1,0:T(4,128)} %bitcast.17, s32[4,128]{1,0:T(4,128)} %bitcast.18, f32[4,128]{1,0:T(4,128)} %bitcast.19, ...), custom_call_target="tpu_custom_call" | custom-call | tf_op jit(solution)/shard_map/backprojection/pallas_call | solution.py:545
  34.0 0.7 %copy.12 = bf16[1,1,128,2,256]{4,3,2,1,0:T(2,128)(2,1)} copy(bf16[1,1,128,2,256]{4,3,2,1,0:T(2,128)(2,1)S(1)} %bitcast.13) | data formatting | bytes 262144

commit v6 on v5

--- a/solution.py
+++ b/solution.py
@@ -171,6 +171,24 @@
             device_id_type=MESH,
         )
 
+    barrier = pltpu.get_barrier_semaphore()
+
+    def greet_col(i, _):
+        pl.semaphore_signal(
+            barrier, inc=1, device_id=(g, row, (col + i) % COLS), device_id_type=MESH
+        )
+        return 0
+
+    def greet_row(i, _):
+        pl.semaphore_signal(
+            barrier, inc=1, device_id=(g, (row + i) % ROWS, col), device_id_type=MESH
+        )
+        return 0
+
+    lax.fori_loop(1, COLS, greet_col, 0)
+    lax.fori_loop(1, ROWS, greet_row, 0)
+    pl.semaphore_signal(barrier, inc=1, device_id=(1 - g, row, col), device_id_type=MESH)
+
     loads = [
         pltpu.make_async_copy(src, dst, in_sems.at[i])
         for i, (src, dst) in enumerate(
@@ -189,24 +207,6 @@
     ]
     for load in loads:
         load.start()
-
-    barrier = pltpu.get_barrier_semaphore()
-
-    def greet_col(i, _):
-        pl.semaphore_signal(
-            barrier, inc=1, device_id=(g, row, (col + i) % COLS), device_id_type=MESH
-        )
-        return 0
-
-    def greet_row(i, _):
-        pl.semaphore_signal(
-            barrier, inc=1, device_id=(g, (row + i) % ROWS, col), device_id_type=MESH
-        )
-        return 0
-
-    lax.fori_loop(1, COLS, greet_col, 0)
-    lax.fori_loop(1, ROWS, greet_row, 0)
-    pl.semaphore_signal(barrier, inc=1, device_id=(1 - g, row, col), device_id_type=MESH)
 
     steps = (iota((8, 256), 0) * iota((8, 256), 1)).astype(F32) * (1.0 / NS)
     tc, ts = cos_sin(steps)
@@ -384,11 +384,9 @@
                 ).wait_recv()
 
     def col_pass(i, part):
-        y = (ry - i + 4) % 4
-        block = pl.ds(pl.multiple_of(y * 4 * SLOTS, 4 * SLOTS), 4 * SLOTS)
         return remote(
-            w_got.at[part, block],
-            w_got.at[part, block],
+            w_got.at[part],
+            w_got.at[part],
             p_send.at[i],
             p_recv.at[i],
             (g, row, col + 1 - 2 * parity),
@@ -411,11 +409,10 @@
         from_cols(wait_z)
         to_owners(m, zall.at[m], slots.at[m], got.at[m])
 
-    for dy in (2, 1, 3, 0):
-        from_rows(2, w_slots, w_got.at[parity], (dy,))
-        c1 = col_pass(dy, parity)
-        c1.start()
-        row_sends.append(c1)
+    from_rows(2, w_slots, w_got.at[parity])
+    c1 = col_pass(0, parity)
+    c1.start()
+    row_sends.append(c1)
 
     for load in loads[4:]:
         load.wait()
@@ -439,8 +436,7 @@
     bank_perm[...] = dot(order, bank_nat[...]).astype(BF16)
 
     weights_t[pl.ds(pl.multiple_of(parity * BEAMS, BEAMS), BEAMS), :] = w_got[parity].T
-    for dy in (2, 1, 3, 0):
-        col_pass(dy, 1 - parity).wait_recv()
+    col_pass(0, 1 - parity).wait_recv()
     weights_t[pl.ds(pl.multiple_of((1 - parity) * BEAMS, BEAMS), BEAMS), :] = w_got[1 - parity].T
 
     def half(bit):

time: 34.8 us -> 35.8 us (1.029)
  the two profiles are of different devices: /device:TPU:1 before, /device:TPU:58 now
where the time goes in v6:
time: 35.8 us
  Pallas kernels  35.1 us (98%)
  local copies, waits for them, and re-layouts  0.66 us (2%)
    pallas_call x1, Pallas kernels, body(): pl.pallas_call(kernel, out_shape=pltpu.VMEM((4 * BEAMS, 128), BF16), in_s...  35.1 us

profile of v6, /device:TPU:58, one launch (start us, length us, event | category | flops | bytes accessed | tf_op | source)
XLA Modules:
  0.0 35.8 jit_solution(13042821857460124244)
XLA Ops:
  0.0 35.1 %backprojection.1 = bf16[512,128]{1,0:T(8,128)(2,1)S(1)} custom-call(bf16[2,32,2048]{2,1,0:T(8,128)(2,1)} %raw_in.1, f32[1,2048]{1,0:T(1,128)} %bitcast.16, bf16[64,128]{1,0:T(8,128)(2,1)} %bitcast.15, s32[1,32]{1,0:T(1,128)} %bitcast.21, s32[4,128]{1,0:T(4,128)} %bitcast.17, s32[4,128]{1,0:T(4,128)} %bitcast.18, f32[4,128]{1,0:T(4,128)} %bitcast.19, ...), custom_call_target="tpu_custom_call" | custom-call | tf_op jit(solution)/shard_map/backprojection/pallas_call | solution.py:541
  35.1 0.7 %copy.12 = bf16[1,1,128,2,256]{4,3,2,1,0:T(2,128)(2,1)} copy(bf16[1,1,128,2,256]{4,3,2,1,0:T(2,128)(2,1)S(1)} %bitcast.13) | data formatting | bytes 262144

commit v7 on v6

--- a/solution.py
+++ b/solution.py
@@ -173,11 +173,10 @@
 
     barrier = pltpu.get_barrier_semaphore()
 
-    def greet_col(i, _):
+    for i in (4, 3, 5, 2, 6, 1, 7):
         pl.semaphore_signal(
             barrier, inc=1, device_id=(g, row, (col + i) % COLS), device_id_type=MESH
         )
-        return 0
 
     def greet_row(i, _):
         pl.semaphore_signal(
@@ -185,7 +184,6 @@
         )
         return 0
 
-    lax.fori_loop(1, COLS, greet_col, 0)
     lax.fori_loop(1, ROWS, greet_row, 0)
     pl.semaphore_signal(barrier, inc=1, device_id=(1 - g, row, col), device_id_type=MESH)
 
@@ -384,9 +382,11 @@
                 ).wait_recv()
 
     def col_pass(i, part):
+        y = (ry - i + 4) % 4
+        block = pl.ds(pl.multiple_of(y * 4 * SLOTS, 4 * SLOTS), 4 * SLOTS)
         return remote(
-            w_got.at[part],
-            w_got.at[part],
+            w_got.at[part, block],
+            w_got.at[part, block],
             p_send.at[i],
             p_recv.at[i],
             (g, row, col + 1 - 2 * parity),
@@ -409,10 +409,11 @@
         from_cols(wait_z)
         to_owners(m, zall.at[m], slots.at[m], got.at[m])
 
-    from_rows(2, w_slots, w_got.at[parity])
-    c1 = col_pass(0, parity)
-    c1.start()
-    row_sends.append(c1)
+    for dy in (2, 1, 3, 0):
+        from_rows(2, w_slots, w_got.at[parity], (dy,))
+        c1 = col_pass(dy, parity)
+        c1.start()
+        row_sends.append(c1)
 
     for load in loads[4:]:
         load.wait()
@@ -436,7 +437,8 @@
     bank_perm[...] = dot(order, bank_nat[...]).astype(BF16)
 
     weights_t[pl.ds(pl.multiple_of(parity * BEAMS, BEAMS), BEAMS), :] = w_got[parity].T
-    col_pass(0, 1 - parity).wait_recv()
+    for dy in (2, 1, 3, 0):
+        col_pass(dy, 1 - parity).wait_recv()
     weights_t[pl.ds(pl.multiple_of((1 - parity) * BEAMS, BEAMS), BEAMS), :] = w_got[1 - parity].T
 
     def half(bit):

time: 35.8 us -> 34.8 us (0.972)
  the two profiles are of different devices: /device:TPU:58 before, /device:TPU:1 now
where the time goes in v7:
time: 34.8 us; the launch traced here: 34.6 us
  Pallas kernels  33.9 us (97%)
  local copies, waits for them, and re-layouts  0.66 us (2%)
    pallas_call x1, Pallas kernels, body(): pl.pallas_call(kernel, out_shape=pltpu.VMEM((4 * BEAMS, 128), BF16), in_s...  33.9 us

profile of v7, /device:TPU:1, one launch (start us, length us, event | category | flops | bytes accessed | tf_op | source)
XLA Modules:
  0.0 34.6 jit_solution(8592800265811787763)
XLA Ops:
  0.0 33.9 %backprojection.1 = bf16[512,128]{1,0:T(8,128)(2,1)S(1)} custom-call(bf16[2,32,2048]{2,1,0:T(8,128)(2,1)} %raw_in.1, f32[1,2048]{1,0:T(1,128)} %bitcast.16, bf16[64,128]{1,0:T(8,128)(2,1)} %bitcast.15, s32[1,32]{1,0:T(1,128)} %bitcast.21, s32[4,128]{1,0:T(4,128)} %bitcast.17, s32[4,128]{1,0:T(4,128)} %bitcast.18, f32[4,128]{1,0:T(4,128)} %bitcast.19, ...), custom_call_target="tpu_custom_call" | custom-call | tf_op jit(solution)/shard_map/backprojection/pallas_call | solution.py:543
  33.9 0.7 %copy.12 = bf16[1,1,128,2,256]{4,3,2,1,0:T(2,128)(2,1)} copy(bf16[1,1,128,2,256]{4,3,2,1,0:T(2,128)(2,1)S(1)} %bitcast.13) | data formatting | bytes 262144
